TPU v7x, 32 devices: a whole 2x2x4 slice. The times are simulated.
32 devices in a mesh: ctx: 16 (over z, y, core), chan: 2 (over x).
Axes of the slice: x: 2, y: 2, z: 4, core: 2. Of those that a mesh axis runs over, the one named last changes fastest.
Arguments:
- query_in: bfloat16 [2048, 1024], P('ctx', 'chan'), may hold values from -6 to 6
- key_in: bfloat16 [2048, 1024], P('ctx', 'chan'), may hold values from -6 to 6
- value_in: bfloat16 [2048, 1024], P('ctx', 'chan'), may hold values from -6 to 6
- grad_out: bfloat16 [2048, 1024], P('ctx', 'chan'), may hold values from -6 to 6
- residue: float32 [16, 1024], P(None, 'chan'), may hold values from -0.34 to 0.34
- decay_rate: float32 [16, 1024], P(None, 'chan'), may hold values from 4.39453125e-05 to 0.05
Outputs:
- grad_query: bfloat16 [2048, 1024], P('ctx', 'chan')
- grad_key: bfloat16 [2048, 1024], P('ctx', 'chan')
- grad_value: bfloat16 [2048, 1024], P('ctx', 'chan')
- grad_residue: float32 [16, 1024], P(None, 'chan')
- grad_log_rate: float32 [16, 1024], P(None, 'chan')
- filter_norm: float32 [], replicated
All inputs are finite; a program needn't handle non-finite values.
Results may differ from a plain program's by a relative error of at most 0.003.
Values may be sent and summed in bfloat16 or wider, within the bound.
A program may use at most 64 MiB of HBM per device.

v0:
```python
import jax
import jax.numpy as jnp
from jax import lax
from jax.sharding import PartitionSpec as P


def forward_combine(early, late):
    return (early[0] * late[0], late[0] * early[1] + late[1])


def backward_combine(right, left):
    right_a, right_b, right_g, right_p = right
    left_a, left_b, left_g, left_p = left
    return (
        left_a * right_a,
        left_a * right_b + left_b * right_a,
        left_a * right_g + left_g,
        left_a * right_p + left_b * right_g + left_p,
    )


def tri_product(matrix, values):
    row_count = values.shape[0]
    flat = values.reshape(row_count, -1)
    out = jnp.dot(matrix, flat, preferred_element_type=jnp.float32, precision=lax.Precision.HIGHEST)
    return out.reshape(values.shape)


def sweep(mixed_in, grad_mix, rates, residues, forward_prefix, backward_prefix):
    row_count = mixed_in.shape[0]
    rows_idx = lax.broadcasted_iota(jnp.int32, (row_count, row_count), 0)
    cols_idx = lax.broadcasted_iota(jnp.int32, (row_count, row_count), 1)
    lower = (rows_idx >= cols_idx).astype(jnp.float32)
    upper = (rows_idx <= cols_idx).astype(jnp.float32)
    lagged = upper * (cols_idx - rows_idx).astype(jnp.float32)
    where_at = jnp.arange(row_count, dtype=jnp.float32)[:, None, None]
    grow = jnp.exp(rates[None] * where_at)
    shrink = jnp.exp(-rates[None] * where_at)
    local_x = tri_product(lower, grow * mixed_in[:, None, :]) * shrink
    span = jnp.exp(-rates * row_count)
    entering = forward_prefix((span, local_x[-1]))[1]
    ahead = where_at + 1.0
    states = local_x + jnp.exp(-rates[None] * ahead) * entering[None]
    conv_part = jnp.sum(residues[None] * states, axis=1)
    weighted = shrink * grad_mix[:, None, :]
    local_g = tri_product(upper, weighted) * grow
    local_p = tri_product(lagged, weighted) * grow
    leaving = backward_prefix((span, row_count * span, local_g[0], local_p[0]))
    behind = jnp.arange(row_count, 0, -1, dtype=jnp.float32)[:, None, None]
    reach = jnp.exp(-rates[None] * behind)
    adjoint = local_g + reach * leaving[2][None]
    second = local_p + reach * leaving[3][None] + behind * reach * leaving[2][None]
    grad_part = jnp.sum(residues[None] * adjoint, axis=1)
    res_sum = jnp.sum(mixed_in[:, None, :] * adjoint, axis=0)
    rate_sum = jnp.sum(mixed_in[:, None, :] * second, axis=0)
    return (conv_part, grad_part, res_sum, rate_sum)


def block_prefix(summary, combine, identity, dev_count, reverse):
    pieces = tuple((part.reshape(part.shape[0], dev_count, -1) for part in summary))
    inclusive = lax.associative_scan(combine, pieces, axis=1, reverse=reverse)
    result = []
    for part, unit in zip(inclusive, identity):
        filler = jnp.full((part.shape[0], 1, part.shape[2]), unit, jnp.float32)
        if reverse:
            shifted = jnp.concatenate([part[:, 1:], filler], 1)
        else:
            shifted = jnp.concatenate([filler, part[:, :-1]], 1)
        result.append(shifted.reshape(part.shape[0], -1))
    return tuple(result)


def on_device(query_in, key_in, value_in, grad_out, residue, decay_rate):
    row_count, chan_count = query_in.shape
    dev_count = lax.axis_size("ctx")
    total_rows = row_count * dev_count
    chan_width = chan_count // dev_count
    stacked = jnp.stack([query_in, key_in, value_in, grad_out]).reshape(
        4, row_count, dev_count, chan_width
    )
    moved = lax.all_to_all(stacked, "ctx", split_axis=2, concat_axis=2, tiled=True).reshape(
        4, row_count, chan_count
    )
    start = lax.axis_index("ctx") * chan_width
    res_lanes = jnp.tile(lax.dynamic_slice_in_dim(residue, start, chan_width, 1), (1, dev_count))
    rate_lanes = jnp.tile(
        lax.dynamic_slice_in_dim(decay_rate, start, chan_width, 1), (1, dev_count)
    )

    def forward_prefix(summary):
        return block_prefix(summary, forward_combine, (1.0, 0.0), dev_count, False)

    def backward_prefix(summary):
        return block_prefix(summary, backward_combine, (1.0, 0.0, 0.0, 0.0), dev_count, True)

    query_local = moved[0].astype(jnp.float32)
    key_local = moved[1].astype(jnp.float32)
    value_local = moved[2].astype(jnp.float32)
    grad_local = moved[3].astype(jnp.float32)
    mixed_in = key_local * value_local
    grad_mix = grad_local * query_local
    conv, grad_conv, res_sum, rate_sum = sweep(
        mixed_in, grad_mix, rate_lanes, res_lanes, forward_prefix, backward_prefix
    )
    results = jnp.stack(
        [
            (grad_local * conv).astype(jnp.bfloat16),
            (grad_conv * value_local).astype(jnp.bfloat16),
            (grad_conv * key_local).astype(jnp.bfloat16),
        ]
    )
    results = results.reshape(3, row_count, dev_count, chan_width)
    returned = lax.all_to_all(results, "ctx", split_axis=2, concat_axis=2, tiled=True).reshape(
        3, row_count, chan_count
    )
    grad_query = returned[0]
    grad_key = returned[1]
    grad_value = returned[2]
    res_sum = jnp.sum(res_sum.reshape(res_sum.shape[0], dev_count, chan_width), axis=1)
    rate_sum = jnp.sum(rate_sum.reshape(rate_sum.shape[0], dev_count, chan_width), axis=1)
    res_full, rate_full = (
        lax.all_gather(res_sum, "ctx", axis=1, tiled=True),
        lax.all_gather(rate_sum, "ctx", axis=1, tiled=True),
    )
    grad_residue = res_full / total_rows
    grad_log_rate = -decay_rate * residue * rate_full / total_rows
    squares = jnp.sum(grad_residue * grad_residue + grad_log_rate * grad_log_rate)
    filter_norm = jnp.sqrt(lax.psum(squares, "chan"))
    return (grad_query, grad_key, grad_value, grad_residue, grad_log_rate, filter_norm)


def solution(mesh):
    return jax.shard_map(
        on_device,
        mesh=mesh,
        in_specs=(
            P("ctx", "chan"),
            P("ctx", "chan"),
            P("ctx", "chan"),
            P("ctx", "chan"),
            P(None, "chan"),
            P(None, "chan"),
        ),
        out_specs=(
            P("ctx", "chan"),
            P("ctx", "chan"),
            P("ctx", "chan"),
            P(None, "chan"),
            P(None, "chan"),
            P(),
        ),
        check_vma=False,
    )
```

profile of v0, /device:TPU:0, one launch (start us, length us, event | category | flops | bytes accessed | tf_op | source)
XLA Modules:
  0.0 116.9 jit_solution(4409055163796792297)
XLA Ops:
  0.7 1.0 copy.124
  1.7 1.0 copy.123
  2.7 1.0 copy.122
  3.8 1.0 copy.121
  4.9 0.8 copy.125
  5.7 7.4 %all-to-all-start = ((bf16[4,128,16,32]{1,3,0,2:T(8,128)(2,1)}), bf16[4,128,16,32]{1,3,0,2:T(8,128)(2,1)S(1)}, u32[]{:S(2)}, u32[]{:S(2)}) async-start(bf16[4,128,16,32]{1,3,0,2:T(8,128)(2,1)} %copy.125), calls=%async_computation | async-start | bytes 1048576 | tf_op jit(solution)/shard_map/all_to_all | solution.py:81
  13.3 0.1 tile.20
  13.5 0.1 tile.18
  13.6 14.0 %all-to-all-done = bf16[4,128,16,32]{1,3,0,2:T(8,128)(2,1)S(1)} async-done(((bf16[4,128,16,32]{1,3,0,2:T(8,128)(2,1)}), bf16[4,128,16,32]{1,3,0,2:T(8,128)(2,1)S(1)}, u32[]{:S(2)}, u32[]{:S(2)}) %all-to-all-start) | async-done | bytes 524320 | tf_op jit(solution)/shard_map/all_to_all | solution.py:81
  27.6 1.2 bitcast_multiply_fusion
  28.8 5.0 %fusion.1 = f32[128,16,512]{2,0,1:T(8,128)} fusion(f32[16,512,128]{2,1,0:T(8,128)S(1)} %bitcast.87, f32[16,512]{1,0:T(8,128)S(1)} %tile.20), kind=kOutput, calls=%fused_computation.9 | convolution fusion | flops 1612726272 | bytes 8421376 | tf_op jit(solution)/shard_map/dot_general | solution.py:25
  33.8 4.4 %fusion = f32[128,16,512]{2,0,1:T(8,128)S(1)} fusion(f32[16,512,128]{2,1,0:T(8,128)S(1)} %bitcast.88, f32[16,512]{1,0:T(8,128)S(1)} %tile.20), kind=kOutput, calls=%fused_computation.8 | convolution fusion | flops 1612775424 | bytes 8421376 | tf_op jit(solution)/shard_map/dot_general | solution.py:25
  38.3 2.0 %copy-done = f32[128,16,512]{2,0,1:T(8,128)} copy-done((f32[128,16,512]{2,0,1:T(8,128)}, f32[128,16,512]{2,0,1:T(8,128)S(1)}, u32[]{:S(2)}) %copy-start) | copy-done | bytes 4194328
  40.5 1.0 slice_reduce_fusion.1
  42.1 0.2 pad.88
  42.4 0.1 copy.129
  42.5 1.2 bitcast_multiply_fusion.1
  43.7 3.2 %exponential_multiply_fusion = f32[128,16,512]{2,0,1:T(8,128)S(1)} fusion(f32[16,512,128]{2,1,0:T(8,128)S(1)} %bitcast.89, f32[16,512]{1,0:T(8,128)S(1)} %neg.23), kind=kOutput, calls=%fused_computation.11 | convolution fusion | flops 1612726272 | bytes 8421376 | tf_op jit(solution)/shard_map/dot_general | solution.py:25
  46.9 2.0 %copy-done.1 = f32[128,16,512]{2,0,1:T(8,128)} copy-done((f32[128,16,512]{2,0,1:T(8,128)}, f32[128,16,512]{2,0,1:T(8,128)S(1)}, u32[]{:S(2)}) %copy-start.1) | copy-done | bytes 4194328
  51.0 6.9 %multiply_reduce_fusion.1 = (f32[16,512]{1,0:T(8,128)S(1)}, f32[128,512]{1,0:T(8,128)S(1)}, f32[16,512]{1,0:T(8,128)S(1)}, f32[128,512]{1,0:T(8,128)S(1)}) fusion(f32[128,16,512]{2,0,1:T(8,128)} %fusion.1, f32[16,512]{1,0:T(8,128)S(1)} %mul.422, f32[128]{0:T(128)S(1)} %get-tuple-element.80, f32[16,512]{1,0:T(8,128)S(1)} %neg.23, f32[128,512]{1,0:T(8,128)S(1)} %copy.129, ...), kind=kLoop, calls=%fused_computation.3 | loop fusion | flops 19775488 | bytes 13599744 | tf_op jit(solution)/shard_map/reduce_sum | solution.py:54
  57.9 0.1 copy.143
  58.0 0.1 copy.136
  58.3 0.8 copy.144
  59.1 4.1 %all-to-all-start.1 = ((bf16[3,128,16,32]{1,3,0,2:T(8,128)(2,1)}), bf16[3,128,16,32]{1,3,0,2:T(8,128)(2,1)S(1)}, u32[]{:S(2)}, u32[]{:S(2)}) async-start(bf16[3,128,16,32]{1,3,0,2:T(8,128)(2,1)} %copy.144), calls=%async_computation.1 | async-start | bytes 786432 | tf_op jit(solution)/shard_map/all_to_all | solution.py:113
  63.3 23.2 %all-gather = f32[16,32,16]{1,2,0:T(8,128)S(1)} all-gather(f32[1,32,16]{1,2,0:T(8,128)S(1)} %bitcast.104), channel_id=1, replica_groups=mesh['ctx'=16,'chan'=2] {'ctx'}, dimensions={0}, use_global_device_ids=true | all-gather | bytes 34816 | tf_op jit(solution)/shard_map/all_gather | solution.py:122
  86.8 19.0 %all-gather.1 = f32[16,32,16]{1,2,0:T(8,128)S(1)} all-gather(f32[1,32,16]{1,2,0:T(8,128)S(1)} %bitcast.103), channel_id=1, replica_groups=mesh['ctx'=16,'chan'=2] {'ctx'}, dimensions={0}, use_global_device_ids=true | all-gather | bytes 34816 | tf_op jit(solution)/shard_map/all_gather | solution.py:123
  105.8 0.1 reshape.148
  105.9 1.2 %add_reduce_fusion = (f32[]{:T(128)}, f32[16,512]{1,0:T(8,128)}) fusion(f32[512,16]{0,1:T(8,128)S(1)} %reshape.148, f32[16,512]{1,0:T(8,128)S(1)} %copy-done.4, f32[16,512]{1,0:T(8,128)S(1)} %copy-done.3, f32[512,16]{0,1:T(8,128)S(1)} %reshape.150), kind=kLoop, calls=%fused_computation.67 | loop fusion | flops 65535 | bytes 163844 | tf_op jit(solution)/shard_map/reduce_sum | solution.py:127
  107.1 5.5 %psum.7 = f32[]{:T(128)} all-reduce(f32[]{:T(128)} %get-tuple-element.34), channel_id=1, replica_groups=mesh['ctx'=16,'chan'=2] {'chan'}, use_global_device_ids=true, to_apply=%region_7.0 | all-reduce | flops 1 | bytes 8 | tf_op jit(solution)/shard_map/psum | solution.py:128
  113.4 0.8 copy.155
  114.2 0.8 copy.156
  115.0 0.8 copy.157
  (123 shorter events, 3.4 us)
Async XLA Ops:
  0.6 12.5 %copy-start.3 = (f32[16,512]{1,0:T(8,128)S(1)}, f32[16,512]{1,0:T(8,128)}, u32[]{:S(2)}) copy-start(f32[16,512]{1,0:T(8,128)} %param.11) | copy-start | bytes 98308
  0.6 12.5 %copy-start.4 = (f32[16,512]{1,0:T(8,128)S(1)}, f32[16,512]{1,0:T(8,128)}, u32[]{:S(2)}) copy-start(f32[16,512]{1,0:T(8,128)} %param.10) | copy-start | bytes 98308
  5.7 21.9 %all-to-all-start = ((bf16[4,128,16,32]{1,3,0,2:T(8,128)(2,1)}), bf16[4,128,16,32]{1,3,0,2:T(8,128)(2,1)S(1)}, u32[]{:S(2)}, u32[]{:S(2)}) async-start(bf16[4,128,16,32]{1,3,0,2:T(8,128)(2,1)} %copy.125), calls=%async_computation | async-start | bytes 1048576 | tf_op jit(solution)/shard_map/all_to_all | solution.py:81
  38.3 2.0 %copy-start = (f32[128,16,512]{2,0,1:T(8,128)}, f32[128,16,512]{2,0,1:T(8,128)S(1)}, u32[]{:S(2)}) copy-start(f32[128,16,512]{2,0,1:T(8,128)S(1)} %fusion) | copy-start | bytes 12582916
  46.9 2.0 %copy-start.1 = (f32[128,16,512]{2,0,1:T(8,128)}, f32[128,16,512]{2,0,1:T(8,128)S(1)}, u32[]{:S(2)}) copy-start(f32[128,16,512]{2,0,1:T(8,128)S(1)} %exponential_multiply_fusion) | copy-start | bytes 12582916
  59.1 54.3 %all-to-all-start.1 = ((bf16[3,128,16,32]{1,3,0,2:T(8,128)(2,1)}), bf16[3,128,16,32]{1,3,0,2:T(8,128)(2,1)S(1)}, u32[]{:S(2)}, u32[]{:S(2)}) async-start(bf16[3,128,16,32]{1,3,0,2:T(8,128)(2,1)} %copy.144), calls=%async_computation.1 | async-start | bytes 786432 | tf_op jit(solution)/shard_map/all_to_all | solution.py:113
  86.6 29.1 %copy-start.2 = (f32[512,16]{0,1:T(8,128)}, f32[512,16]{0,1:T(8,128)S(1)}, u32[]{:S(2)}) copy-start(f32[512,16]{0,1:T(8,128)S(1)} %reshape.150) | copy-start | bytes 98308
where the time goes:
time: 117 us
  blocking collectives  47.7 us (41%)
  local copies, waits for them, and re-layouts  16.4 us (14%)
  waiting for transfers between devices  14 us (12%)
  matrix products  12.7 us (11%)
  starting transfers between devices  11.5 us (10%)
  other arithmetic  11.3 us (10%)
  between operations  3.41 us (3%)
    all_gather x1, blocking collectives, on_device(): lax.all_gather(res_sum, 'ctx', axis=1, tiled=True)  23.2 us
    all_gather x1, blocking collectives, on_device(): lax.all_gather(rate_sum, 'ctx', axis=1, tiled=True)  19 us
    all_to_all x1, waiting for transfers between devices, on_device(): lax.all_to_all(stacked, 'ctx', split_axis=2, concat_axis=2, tiled=True)  14 us
    dot_general x3, matrix products, tri_product(): jnp.dot(matrix, flat, preferred_element_type=jnp.float32, precision=lax.P...  12.7 us
    unnamed x30, local copies, waits for them, and re-layouts  10.9 us
    all_to_all x1, starting transfers between devices, on_device(): lax.all_to_all(stacked, 'ctx', split_axis=2, concat_axis=2, tiled=True)  7.39 us
    reduce_sum x1, other arithmetic, sweep(): res_sum = jnp.sum(mixed_in[:, None, :] * adjoint, axis=0)  6.86 us
    psum x1, blocking collectives, on_device(): filter_norm = jnp.sqrt(lax.psum(squares, 'chan'))  5.55 us
  transfers between devices with their start and end apart: 2, of which 1 were waited for; matrix products, arithmetic and copies ran while one was open for 2% of the time, Pallas kernels for 0%

commit v1 on v0

v1 whole, which is shorter than its diff:
```python
import functools

import jax
import jax.numpy as jnp
from jax import lax
from jax.experimental import pallas as pl
from jax.experimental.pallas import tpu as pltpu
from jax.sharding import PartitionSpec as P

MESH = pl.DeviceIdType.MESH
LANES = 128
SUBS = 8
ROWS = 6
GROUP = 4


def local_kernel(
    query_ref, key_ref, value_ref, grad_ref, res_ref, rate_ref,
    sum_ref, span_ref, enter_ref, leave_ref, conv_ref, gconv_ref,
    mixed, gmix, tables,
):
    tile = pl.program_id(0)
    tiles = pl.num_programs(0)
    rows = mixed.shape[0]
    block = rows // SUBS
    modes = res_ref.shape[0]
    mixed[...] = key_ref[...].astype(jnp.float32) * value_ref[...].astype(jnp.float32)
    gmix[...] = grad_ref[...].astype(jnp.float32) * query_ref[...].astype(jnp.float32)
    x = [mixed[pl.ds(i, SUBS, stride=block), :] for i in range(block)]
    g = [gmix[pl.ds(i, SUBS, stride=block), :] for i in range(block)]
    rate = rate_ref[...]
    factor = jnp.exp(-rate)
    res = res_ref[...]
    power = jnp.ones_like(factor)
    taps = []
    lag_res = jnp.zeros_like(factor)
    lag_rate = jnp.zeros_like(factor)
    for j in range(block):
        taps.append(jnp.sum(res * power, axis=0, keepdims=True))
        products = x[0] * g[j]
        for i in range(1, block - j):
            products = products + x[i] * g[i + j]
        term = power * jnp.sum(products, axis=0, keepdims=True)
        lag_res = lag_res + term
        lag_rate = lag_rate + float(j) * term
        power = power * factor
    taps = [jnp.broadcast_to(h, (SUBS, LANES)) for h in taps]
    for i in range(block):
        total = taps[0] * x[i]
        for j in range(1, i + 1):
            total = total + taps[j] * x[i - j]
        conv_ref[i] = total
        total = taps[0] * g[i]
        for j in range(1, block - i):
            total = total + taps[j] * g[i + j]
        gconv_ref[i] = total
    tables[0] = factor
    tables[1] = rate
    tables[2] = lag_res
    tables[3] = lag_rate
    sub = lax.broadcasted_iota(jnp.int32, (SUBS, LANES), 0)
    before = sub.astype(jnp.float32) * float(block)
    after = (SUBS - 1 - sub).astype(jnp.float32) * float(block)

    def one_mode(m):
        f = jnp.broadcast_to(tables[0, pl.ds(m, 1), :], (SUBS, LANES))
        r = jnp.broadcast_to(tables[1, pl.ds(m, 1), :], (SUBS, LANES))
        head = x[0] * f
        head1 = head
        for i in range(1, block):
            head = (head + x[i]) * f
            head1 = head1 * f + head
        tail = g[block - 1]
        tail1 = jnp.zeros_like(tail)
        for i in range(block - 2, -1, -1):
            tail1 = (tail1 + tail) * f
            tail = tail * f + g[i]
        step = jnp.exp(r * -float(block))
        up, down, weight = head, tail, step
        for shift in (1, 2, 4):
            up = up + jnp.where(sub >= shift, weight * pltpu.roll(up, shift, 0), 0.0)
            down = down + jnp.where(
                sub < SUBS - shift, weight * pltpu.roll(down, SUBS - shift, 0), 0.0
            )
            weight = weight * weight
        enter = jnp.where(sub >= 1, pltpu.roll(up, 1, 0), 0.0)
        leave = jnp.where(sub < SUBS - 1, pltpu.roll(down, SUBS - 1, 0), 0.0)
        enter_ref[m] = enter
        leave_ref[m] = leave
        moment = jnp.exp(-r * after) * (head1 + after * head)
        gmoment = jnp.exp(-r * before) * (tail1 + before * tail)
        cross = head * leave
        cross1 = head1 * leave + enter * (tail1 + float(block) * step * leave)
        found = (
            up[SUBS - 1 :],
            down[:1],
            jnp.sum(moment, axis=0, keepdims=True),
            jnp.sum(gmoment, axis=0, keepdims=True),
            jnp.sum(cross, axis=0, keepdims=True) + tables[2, pl.ds(m, 1), :],
            jnp.sum(cross1, axis=0, keepdims=True) + tables[3, pl.ds(m, 1), :],
        )
        for at, row in enumerate(found):
            sum_ref[m, pl.ds(at * tiles + tile, 1), :] = row
        span_ref[m, pl.ds(tile, 1), :] = weight[:1]

    @pl.loop(0, modes // GROUP)
    def _(at):
        for lane in range(GROUP):
            one_mode(at * GROUP + lane)


def exchange_kernel(
    ctx, chan, positions,
    sum_ref, span_ref, res_ref, rate_ref,
    edge_ref, gres_ref, grate_ref, norm_ref,
    inbox, outbox, answer, square, send1, recv1, send2, recv2, send3, recv3,
):
    modes, width = sum_ref.shape[0], sum_ref.shape[1]
    tiles = width // ROWS
    rows = positions // ctx
    stride = ctx // modes
    me = lax.axis_index("ctx")
    mine = lax.axis_index("chan")
    mode = me // stride

    barrier = pltpu.get_barrier_semaphore()

    @pl.loop(1, ctx)
    def _(p):
        pl.semaphore_signal(
            barrier, inc=1, device_id=(lax.rem(me + p, ctx), mine), device_id_type=MESH
        )

    for p in range(1, chan):
        pl.semaphore_signal(
            barrier, inc=1, device_id=(me, lax.rem(mine + p, chan)), device_id_type=MESH
        )
    pl.semaphore_wait(barrier, ctx - 1 + chan - 1)

    def ask(m, slot, target):
        return pltpu.make_async_remote_copy(
            src_ref=sum_ref.at[m],
            dst_ref=inbox.at[slot],
            send_sem=send1.at[m],
            recv_sem=recv1.at[slot],
            device_id=(target, mine),
            device_id_type=MESH,
        )

    def reply(d, slot, target):
        return pltpu.make_async_remote_copy(
            src_ref=outbox.at[d],
            dst_ref=answer.at[slot],
            send_sem=send2.at[d],
            recv_sem=recv2.at[slot],
            device_id=(target, mine),
            device_id_type=MESH,
        )

    def owner_work():
        inbox[me] = sum_ref[mode]

        @pl.loop(1, ctx)
        def _(p):
            d = lax.rem(me + p, ctx)
            ask(mode, d, d).wait_recv()

        span = span_ref[mode]
        enter = jnp.zeros_like(span)
        for d in range(ctx):
            outbox[d, 0:tiles, :] = enter
            enter = span * enter + inbox[d, 0:tiles, :]
        leave = jnp.zeros_like(span)
        res_total = jnp.zeros_like(span)
        rate_total = jnp.zeros_like(span)
        for d in range(ctx - 1, -1, -1):
            outbox[d, tiles : 2 * tiles, :] = leave
            into = outbox[d, 0:tiles, :]
            head = inbox[d, 0:tiles, :]
            tail = inbox[d, tiles : 2 * tiles, :]
            head1 = inbox[d, 2 * tiles : 3 * tiles, :]
            tail1 = inbox[d, 3 * tiles : 4 * tiles, :]
            res_total = res_total + (inbox[d, 4 * tiles : 5 * tiles, :] + head * leave)
            rate_total = rate_total + (
                inbox[d, 5 * tiles : 6 * tiles, :]
                + head1 * leave
                + into * (tail1 + float(rows) * span * leave)
            )
            leave = span * leave + tail
        for d in range(ctx):
            outbox[d, 2 * tiles : 3 * tiles, :] = res_total
            outbox[d, 3 * tiles : 4 * tiles, :] = rate_total

        @pl.loop(1, ctx)
        def _(p):
            d = lax.rem(me + p, ctx)
            reply(d, mode, d).start()

        answer[mode] = outbox[me]

    @pl.loop(1, modes)
    def _(p):
        m = lax.rem(mode + p, modes)
        ask(m, me, m * stride).start()

    if stride == 1:
        owner_work()
    else:
        owner = lax.rem(me, stride) == 0
        pl.when(jnp.logical_not(owner))(lambda: ask(mode, me, mode * stride).start())
        pl.when(owner)(owner_work)
        pl.when(jnp.logical_not(owner))(
            lambda: reply(me, mode, mode * stride).wait_recv()
        )

    @pl.loop(1, modes)
    def _(p):
        m = lax.rem(mode + p, modes)
        reply(me, m, m * stride).wait_recv()

    edge_ref[...] = answer[:, 0 : 2 * tiles, :]
    total = jnp.zeros((1, LANES), jnp.float32)
    for t in range(tiles):
        lanes = slice(t * LANES, (t + 1) * LANES)
        grad_res = answer[:, 2 * tiles + t, :] / positions
        grad_rate = (
            -rate_ref[:, lanes] * res_ref[:, lanes] * answer[:, 3 * tiles + t, :] / positions
        )
        gres_ref[:, lanes] = grad_res
        grate_ref[:, lanes] = grad_rate
        total = total + jnp.sum(
            grad_res * grad_res + grad_rate * grad_rate, axis=0, keepdims=True
        )
    square[0] = jnp.broadcast_to(total, (SUBS, LANES))

    def partner(p):
        return pltpu.make_async_remote_copy(
            src_ref=square.at[0],
            dst_ref=square.at[p],
            send_sem=send3.at[p],
            recv_sem=recv3.at[p],
            device_id=(me, lax.rem(mine + p, chan)),
            device_id_type=MESH,
        )

    for p in range(1, chan):
        partner(p).start()
    for p in range(1, chan):
        partner(p).wait_recv()
    whole = jnp.sum(square[...], axis=0)[:1]
    norm_ref[...] = jnp.sqrt(jnp.sum(whole, axis=1, keepdims=True))

    for p in range(1, chan):
        partner(p).wait_send()

    @pl.loop(1, modes)
    def _(p):
        m = lax.rem(mode + p, modes)
        ask(m, me, m * stride).wait_send()

    def drain():
        @pl.loop(1, ctx)
        def _(p):
            d = lax.rem(me + p, ctx)
            reply(d, mode, d).wait_send()

    if stride == 1:
        drain()
    else:
        owner = lax.rem(me, stride) == 0
        pl.when(jnp.logical_not(owner))(
            lambda: ask(mode, me, mode * stride).wait_send()
        )
        pl.when(owner)(drain)


def finish_kernel(
    query_ref, key_ref, value_ref, grad_ref, res_ref, rate_ref,
    edge_ref, enter_ref, leave_ref, conv_ref, gconv_ref,
    gq_ref, gk_ref, gv_ref,
    full, gfull, tables,
):
    tile = pl.program_id(0)
    tiles = pl.num_programs(0)
    rows = full.shape[0]
    block = rows // SUBS
    modes = res_ref.shape[0]
    tables[0] = jnp.exp(-rate_ref[...])
    sub = lax.broadcasted_iota(jnp.int32, (SUBS, LANES), 0)
    before = sub.astype(jnp.float32) * float(block)
    after = (SUBS - 1 - sub).astype(jnp.float32) * float(block)

    def body(at, held):
        conv, gconv = list(held[0]), list(held[1])
        for lane in range(GROUP):
            m = at * GROUP + lane
            f = jnp.broadcast_to(tables[0, pl.ds(m, 1), :], (SUBS, LANES))
            rate = rate_ref[pl.ds(m, 1), :]
            res = res_ref[pl.ds(m, 1), :]
            into = edge_ref[m, pl.ds(tile, 1), :]
            out = edge_ref[m, pl.ds(tiles + tile, 1), :]
            z = res * (enter_ref[m] + jnp.exp(-rate * before) * into)
            y = (res * f) * (leave_ref[m] + jnp.exp(-rate * after) * out)
            for i in range(block):
                conv[i] = conv[i] + z
                gconv[block - 1 - i] = gconv[block - 1 - i] + y
                if i < block - 1:
                    z = z * f
                    y = y * f
        return tuple(conv), tuple(gconv)

    start = (
        tuple(conv_ref[i] for i in range(block)),
        tuple(gconv_ref[i] for i in range(block)),
    )
    conv, gconv = lax.fori_loop(0, modes // GROUP, body, start)
    for i in range(block):
        full[pl.ds(i, SUBS, stride=block), :] = conv[i]
        gfull[pl.ds(i, SUBS, stride=block), :] = gconv[i]
    gq_ref[...] = (grad_ref[...].astype(jnp.float32) * full[...]).astype(jnp.bfloat16)
    gk_ref[...] = (gfull[...] * value_ref[...].astype(jnp.float32)).astype(jnp.bfloat16)
    gv_ref[...] = (gfull[...] * key_ref[...].astype(jnp.float32)).astype(jnp.bfloat16)


def on_device(ctx, chan, query_in, key_in, value_in, grad_out, residue, decay_rate):
    rows, channels = query_in.shape
    modes = residue.shape[0]
    tiles = channels // LANES
    block = rows // SUBS
    f32 = jnp.float32
    data = pl.BlockSpec((rows, LANES), lambda t: (0, t))
    param = pl.BlockSpec((modes, LANES), lambda t: (0, t))
    state = pl.BlockSpec((modes, SUBS, LANES), lambda t: (0, 0, t))
    local = pl.BlockSpec((block, SUBS, LANES), lambda t: (0, 0, t))

    def whole(shape):
        return pl.BlockSpec(shape, lambda t: (0,) * len(shape))

    sums, spans, enter, leave, conv, gconv = pl.pallas_call(
        local_kernel,
        grid=(tiles,),
        in_specs=[data] * 4 + [param] * 2,
        out_specs=[
            whole((modes, ROWS * tiles, LANES)),
            whole((modes, tiles, LANES)),
            state, state, local, local,
        ],
        out_shape=[
            jax.ShapeDtypeStruct((modes, ROWS * tiles, LANES), f32),
            jax.ShapeDtypeStruct((modes, tiles, LANES), f32),
            jax.ShapeDtypeStruct((modes, SUBS, channels), f32),
            jax.ShapeDtypeStruct((modes, SUBS, channels), f32),
            jax.ShapeDtypeStruct((block, SUBS, channels), f32),
            jax.ShapeDtypeStruct((block, SUBS, channels), f32),
        ],
        scratch_shapes=[
            pltpu.VMEM((rows, LANES), f32),
            pltpu.VMEM((rows, LANES), f32),
            pltpu.VMEM((4, modes, LANES), f32),
        ],
        name="local",
    )(query_in, key_in, value_in, grad_out, residue, decay_rate)

    vmem = pl.BlockSpec(memory_space=pltpu.VMEM)
    dma = pltpu.SemaphoreType.DMA
    edges, grad_residue, grad_log_rate, norm = pl.pallas_call(
        functools.partial(exchange_kernel, ctx, chan, rows * ctx),
        in_specs=[vmem] * 4,
        out_specs=[vmem] * 4,
        out_shape=[
            jax.ShapeDtypeStruct((modes, 2 * tiles, LANES), f32),
            jax.ShapeDtypeStruct((modes, channels), f32),
            jax.ShapeDtypeStruct((modes, channels), f32),
            jax.ShapeDtypeStruct((1, 1), f32),
        ],
        scratch_shapes=[
            pltpu.VMEM((ctx, ROWS * tiles, LANES), f32),
            pltpu.VMEM((ctx, 4 * tiles, LANES), f32),
            pltpu.VMEM((modes, 4 * tiles, LANES), f32),
            pltpu.VMEM((chan, SUBS, LANES), f32),
            dma((modes,)), dma((ctx,)), dma((ctx,)), dma((modes,)),
            dma((chan,)), dma((chan,)),
        ],
        compiler_params=pltpu.CompilerParams(collective_id=0, has_side_effects=True),
        name="exchange",
    )(sums, spans, residue, decay_rate)

    grads = pl.pallas_call(
        finish_kernel,
        grid=(tiles,),
        in_specs=[data] * 4 + [param] * 2
        + [whole((modes, 2 * tiles, LANES)), state, state, local, local],
        out_specs=[data] * 3,
        out_shape=[jax.ShapeDtypeStruct((rows, channels), jnp.bfloat16)] * 3,
        scratch_shapes=[
            pltpu.VMEM((rows, LANES), f32),
            pltpu.VMEM((rows, LANES), f32),
            pltpu.VMEM((1, modes, LANES), f32),
        ],
        name="finish",
    )(
        query_in, key_in, value_in, grad_out, residue, decay_rate,
        edges, enter, leave, conv, gconv,
    )
    return (*grads, grad_residue, grad_log_rate, norm.reshape(()))


def solution(mesh):
    return jax.shard_map(
        functools.partial(on_device, mesh.shape["ctx"], mesh.shape["chan"]),
        mesh=mesh,
        in_specs=(P("ctx", "chan"),) * 4 + (P(None, "chan"),) * 2,
        out_specs=(P("ctx", "chan"),) * 3 + (P(None, "chan"),) * 2 + (P(),),
        check_vma=False,
    )
```

time: 117 us -> 35.7 us (0.31)
  blocking collectives: 47.7 us -> 0 us
  Pallas kernels: 0 us -> 31.2 us
  local copies, waits for them, and re-layouts: 16.4 us -> 1.37 us
  waiting for transfers between devices: 14 us -> 0 us
  matrix products: 12.7 us -> 0 us
  starting transfers between devices: 11.5 us -> 0 us
  other arithmetic: 11.3 us -> 0 us
    all_gather x2 -> x0, blocking collectives: 42.2 us -> none  [the longest x1 23.2 us: on_device(): lax.all_gather(res_sum, 'ctx', axis=1, tiled=True)]
    pallas_call x0 -> x3, Pallas kernels: none -> 31.2 us  [the longest x1 22.4 us: on_device(): pl.pallas_call(functools.partial(exchange_kernel, ctx, chan, rows * ctx),...]
    all_to_all x2 -> x0, waiting for transfers between devices: 14 us -> none  [the longest x1 14 us: on_device(): lax.all_to_all(stacked, 'ctx', split_axis=2, concat_axis=2, tiled=True)]
    dot_general x3 -> x0, matrix products: 12.7 us -> none  [tri_product(): jnp.dot(matrix, flat, preferred_element_type=jnp.float32, precision=lax.P...]
    all_to_all x2 -> x0, starting transfers between devices: 11.5 us -> none  [the longest x1 7.39 us: on_device(): lax.all_to_all(stacked, 'ctx', split_axis=2, concat_axis=2, tiled=True)]
    unnamed x30 -> x6, local copies, waits for them, and re-layouts: 10.9 us -> 1.37 us
    reduce_sum x4 -> x0, other arithmetic: 8.14 us -> none  [the longest x1 6.86 us: sweep(): res_sum = jnp.sum(mixed_in[:, None, :] * adjoint, axis=0)]
    psum x1 -> x0, blocking collectives: 5.55 us -> none  [on_device(): filter_norm = jnp.sqrt(lax.psum(squares, 'chan'))]
  transfers between devices with their start and end apart: 2 -> 0, of which waited for: 1 -> 0; matrix products, arithmetic and copies ran while one was open for 2% -> 0% of each run, Pallas kernels for 0% -> 0%
where the time goes in v1:
time: 35.7 us; the launch traced here: 35 us
  Pallas kernels  31.2 us (87%)
  between operations  2.43 us (7%)
  local copies, waits for them, and re-layouts  1.37 us (4%)
    pallas_call x1, Pallas kernels, on_device(): pl.pallas_call(functools.partial(exchange_kernel, ctx, chan, rows * ctx),...  22.4 us
    pallas_call x1, Pallas kernels, on_device(): pl.pallas_call(local_kernel, grid=(tiles,), in_specs=[data] * 4 + [param]...  4.73 us
    pallas_call x1, Pallas kernels, on_device(): pl.pallas_call(finish_kernel, grid=(tiles,), in_specs=[data] * 4 + [param...  4.09 us
    unnamed x6, local copies, waits for them, and re-layouts  1.37 us

profile of v1, /device:TPU:0, one launch (start us, length us, event | category | flops | bytes accessed | tf_op | source)
XLA Modules:
  0.0 35.0 jit_solution(976121361289329721)
XLA Ops:
  0.6 4.7 %local.1 = (f32[16,24,128]{2,1,0:T(8,128)}, f32[16,4,128]{2,1,0:T(4,128)}, f32[16,8,512]{2,1,0:T(8,128)}, f32[16,8,512]{2,1,0:T(8,128)}, f32[16,8,512]{2,1,0:T(8,128)}, /*index=5*/f32[16,8,512]{2,1,0:T(8,128)}) custom-call(bf16[128,512]{1,0:T(8,128)(2,1)} %query_ref.3, bf16[128,512]{1,0:T(8,128)(2,1)} %key_ref.3, bf16[128,512]{1,0:T(8,128)(2,1)} %value_ref.3, ...), custom_call_target="tpu_custom_call" | custom-call | tf_op jit(solution)/shard_map/local/pallas_call | solution.py:339
  5.4 22.4 %exchange.1 = (f32[16,8,128]{2,1,0:T(8,128)}, f32[16,512]{1,0:T(8,128)}, f32[16,512]{1,0:T(8,128)}, f32[1,1]{1,0:T(1,128)}) custom-call(f32[16,24,128]{2,1,0:T(8,128)} %get-tuple-element.19.sum_ref, f32[16,4,128]{2,1,0:T(4,128)} %get-tuple-element.20.span_ref, f32[16,512]{1,0:T(8,128)} %res_ref.5, f32[16,512]{1,0:T(8,128)} %rate_ref.5), custom_call_target="tpu_custom_call" | custom-call | tf_op jit(solution)/shard_map/exchange/pallas_call | solution.py:366
  27.7 0.0 copy-start.1
  27.7 4.1 %finish.1 = (bf16[128,512]{1,0:T(8,128)(2,1)}, bf16[128,512]{1,0:T(8,128)(2,1)}, bf16[128,512]{1,0:T(8,128)(2,1)}) custom-call(bf16[128,512]{1,0:T(8,128)(2,1)} %query_ref.3, bf16[128,512]{1,0:T(8,128)(2,1)} %key_ref.3, bf16[128,512]{1,0:T(8,128)(2,1)} %value_ref.3, bf16[128,512]{1,0:T(8,128)(2,1)} %grad_ref.3, f32[16,512]{1,0:T(8,128)} %res_ref.5, ...), custom_call_target="tpu_custom_call" | custom-call | tf_op jit(solution)/shard_map/finish/pallas_call | solution.py:388
  31.8 0.0 copy-done.1
  31.8 0.0 copy-start
  31.9 0.6 %copy.15 = f32[16,512]{1,0:T(8,128)} copy(f32[16,512]{1,0:T(8,128)S(1)} %copy-done.1) | data formatting | bytes 65536
  32.5 0.1 copy-done
  32.6 0.6 %copy.16 = f32[16,512]{1,0:T(8,128)} copy(f32[16,512]{1,0:T(8,128)S(1)} %copy-done) | data formatting | bytes 65536
Async XLA Ops:
  27.7 4.1 %copy-start.1 = (f32[16,512]{1,0:T(8,128)S(1)}, f32[16,512]{1,0:T(8,128)}, u32[]{:S(2)}) copy-start(f32[16,512]{1,0:T(8,128)} %get-tuple-element.41) | copy-start | bytes 98308
  31.8 0.8 %copy-start = (f32[16,512]{1,0:T(8,128)S(1)}, f32[16,512]{1,0:T(8,128)}, u32[]{:S(2)}) copy-start(f32[16,512]{1,0:T(8,128)} %get-tuple-element.42) | copy-start | bytes 98308

commit v2 on v0

v2 whole, which is shorter than its diff:
```python
import functools

import jax
import jax.numpy as jnp
from jax import lax
from jax.experimental import pallas as pl
from jax.experimental.pallas import tpu as pltpu
from jax.sharding import PartitionSpec as P

MESH = pl.DeviceIdType.MESH
LANES = 128
SUBS = 8
GROUP = 4


def kernel(
    ctx, chan, positions,
    query_ref, key_ref, value_ref, grad_ref, res_ref, rate_ref,
    gq_ref, gk_ref, gv_ref, gres_ref, grate_ref, norm_ref,
    mixed, gmix, factors, rates, residues, lags, enters, leaves, convs, gconvs, moments, locals_, spans,
    sums, inbox, outbox, edges, parts, partbox, total, answer, square,
    send1, recv1, send2, recv2, send3, recv3, send4, recv4, send5, recv5,
):
    modes, channels = res_ref.shape
    tiles = channels // LANES
    rows = query_ref.shape[0]
    block = rows // SUBS
    stride = ctx // modes
    me = lax.axis_index("ctx")
    mine = lax.axis_index("chan")
    mode = me // stride
    f32 = jnp.float32

    barrier = pltpu.get_barrier_semaphore()

    @pl.loop(1, ctx)
    def _(p):
        pl.semaphore_signal(
            barrier, inc=1, device_id=(lax.rem(me + p, ctx), mine), device_id_type=MESH
        )

    for p in range(1, chan):
        pl.semaphore_signal(
            barrier, inc=1, device_id=(me, lax.rem(mine + p, chan)), device_id_type=MESH
        )

    sub = lax.broadcasted_iota(jnp.int32, (SUBS, LANES), 0)
    before = sub.astype(f32) * float(block)
    after = (SUBS - 1 - sub).astype(f32) * float(block)

    def lanes_of(t):
        return pl.ds(pl.multiple_of(t * LANES, LANES), LANES)

    def blocks_of(ref, t):
        return [ref[t, pl.ds(i, SUBS, stride=block), :] for i in range(block)]

    def row_of(ref, m, t):
        return jnp.broadcast_to(ref[t, pl.ds(m, 1), :], (SUBS, LANES))

    @pl.loop(0, tiles)
    def _(t):
        lanes = lanes_of(t)
        mixed[t] = key_ref[:, lanes].astype(f32) * value_ref[:, lanes].astype(f32)
        gmix[t] = grad_ref[:, lanes].astype(f32) * query_ref[:, lanes].astype(f32)
        rates[t] = rate_ref[:, lanes]
        residues[t] = res_ref[:, lanes]
        factors[t] = jnp.exp(-rates[t])
        x = blocks_of(mixed, t)
        g = blocks_of(gmix, t)

        @pl.loop(0, modes // GROUP)
        def _(at):
            for lane in range(GROUP):
                m = at * GROUP + lane
                f = row_of(factors, m, t)
                head = x[0] * f
                tail = g[block - 1]
                for i in range(1, block):
                    head = (head + x[i]) * f
                    tail = tail * f + g[block - 1 - i]
                weight = f
                for _ in range(block.bit_length() - 1):
                    weight = weight * weight
                up, down = head, tail
                for shift in (1, 2, 4):
                    up = up + jnp.where(sub >= shift, weight * pltpu.roll(up, shift, 0), 0.0)
                    down = down + jnp.where(
                        sub < SUBS - shift, weight * pltpu.roll(down, SUBS - shift, 0), 0.0
                    )
                    weight = weight * weight
                enters[m, t] = jnp.where(sub >= 1, pltpu.roll(up, 1, 0), 0.0)
                leaves[m, t] = jnp.where(sub < SUBS - 1, pltpu.roll(down, SUBS - 1, 0), 0.0)
                sums[m, pl.ds(t, 1), :] = up[SUBS - 1 :]
                sums[m, pl.ds(tiles + t, 1), :] = down[:1]
                spans[m, pl.ds(t, 1), :] = weight[:1]

    pl.semaphore_wait(barrier, ctx - 1 + chan - 1)

    def to_owner(src, dst, sends, recvs, m, slot, target):
        return pltpu.make_async_remote_copy(
            src_ref=src.at[m],
            dst_ref=dst.at[slot],
            send_sem=sends.at[m],
            recv_sem=recvs.at[slot],
            device_id=(target, mine),
            device_id_type=MESH,
        )

    def from_owner(src, dst, sends, recvs, d, slot, target):
        return pltpu.make_async_remote_copy(
            src_ref=src.at[d] if src is outbox else src,
            dst_ref=dst.at[slot],
            send_sem=sends.at[d],
            recv_sem=recvs.at[slot],
            device_id=(target, mine),
            device_id_type=MESH,
        )

    ask = functools.partial(to_owner, sums, inbox, send1, recv1)
    reply = functools.partial(from_owner, outbox, edges, send2, recv2)
    give = functools.partial(to_owner, parts, partbox, send3, recv3)
    spread = functools.partial(from_owner, total, answer, send4, recv4)

    def if_owner(then, otherwise=None):
        if stride == 1:
            then()
            return
        owner = lax.rem(me, stride) == 0
        pl.when(owner)(then)
        if otherwise is not None:
            pl.when(jnp.logical_not(owner))(otherwise)

    def each_mode(act):
        @pl.loop(1, modes)
        def _(p):
            act(lax.rem(mode + p, modes))

    def each_peer(act):
        @pl.loop(1, ctx)
        def _(p):
            act(lax.rem(me + p, ctx))

    each_mode(lambda m: ask(m, me, m * stride).start())
    if_owner(lambda: None, lambda: ask(mode, me, mode * stride).start())

    @pl.loop(0, tiles)
    def _(t):
        lanes = lanes_of(t)
        x = blocks_of(mixed, t)
        g = blocks_of(gmix, t)
        factor = factors[t]
        res = residues[t]
        power = jnp.ones_like(factor)
        taps = []
        lag_res = jnp.zeros_like(factor)
        lag_rate = jnp.zeros_like(factor)
        for j in range(block):
            tap = jnp.sum(res * power, axis=0, keepdims=True)
            taps.append(jnp.broadcast_to(tap, (SUBS, LANES)))
            products = x[0] * g[j]
            for i in range(1, block - j):
                products = products + x[i] * g[i + j]
            term = power * jnp.sum(products, axis=0, keepdims=True)
            lag_res = lag_res + term
            lag_rate = lag_rate + float(j) * term
            power = power * factor
        for i in range(block):
            acc = taps[0] * x[i]
            for j in range(1, i + 1):
                acc = acc + taps[j] * x[i - j]
            convs[t, i] = acc
            acc = taps[0] * g[i]
            for j in range(1, block - i):
                acc = acc + taps[j] * g[i + j]
            gconvs[t, i] = acc
        lags[0] = lag_res
        lags[1] = lag_rate

        @pl.loop(0, modes // GROUP)
        def _(at):
            for lane in range(GROUP):
                m = at * GROUP + lane
                f = row_of(factors, m, t)
                head = x[0] * f
                head1 = head
                tail = g[block - 1]
                tail1 = jnp.zeros_like(tail)
                for i in range(1, block):
                    head = (head + x[i]) * f
                    head1 = head1 * f + head
                    tail1 = (tail1 + tail) * f
                    tail = tail * f + g[block - 1 - i]
                rate = rates[t, pl.ds(m, 1), :]
                enter = enters[m, t]
                leave = leaves[m, t]
                step = jnp.exp(rate * -float(block))
                moment = jnp.exp(-rate * after) * (head1 + after * head)
                gmoment = jnp.exp(-rate * before) * (tail1 + before * tail)
                cross = head * leave
                cross1 = head1 * leave + enter * (tail1 + float(block) * step * leave)
                moments[m, pl.ds(t, 1), :] = jnp.sum(moment, axis=0, keepdims=True)
                moments[m, pl.ds(tiles + t, 1), :] = jnp.sum(gmoment, axis=0, keepdims=True)
                locals_[m, pl.ds(t, 1), :] = (
                    jnp.sum(cross, axis=0, keepdims=True) + lags[0, pl.ds(m, 1), :]
                )
                locals_[m, pl.ds(tiles + t, 1), :] = (
                    jnp.sum(cross1, axis=0, keepdims=True) + lags[1, pl.ds(m, 1), :]
                )

    def owner_prefix():
        inbox[me] = sums[mode]
        each_peer(lambda d: ask(mode, d, d).wait_recv())
        span = spans[mode]
        enter = jnp.zeros_like(span)
        leave = jnp.zeros_like(span)
        for d in range(ctx):
            outbox[d, 0:tiles, :] = enter
            enter = span * enter + inbox[d, 0:tiles, :]
            back = ctx - 1 - d
            outbox[back, tiles : 2 * tiles, :] = leave
            leave = span * leave + inbox[back, tiles : 2 * tiles, :]
        each_peer(lambda d: reply(d, mode, d).start())
        edges[mode] = outbox[me]

    if_owner(owner_prefix, lambda: reply(me, mode, mode * stride).wait_recv())
    each_mode(lambda m: reply(me, m, m * stride).wait_recv())

    enter = edges[:, 0:tiles, :]
    leave = edges[:, tiles : 2 * tiles, :]
    parts[:, 0:tiles, :] = locals_[:, 0:tiles, :] + sums[:, 0:tiles, :] * leave
    parts[:, tiles : 2 * tiles, :] = (
        locals_[:, tiles : 2 * tiles, :]
        + moments[:, 0:tiles, :] * leave
        + enter * (moments[:, tiles : 2 * tiles, :] + float(rows) * spans[...] * leave)
    )
    each_mode(lambda m: give(m, me, m * stride).start())
    if_owner(lambda: None, lambda: give(mode, me, mode * stride).start())

    def finish(t):
        lanes = lanes_of(t)

        def body(at, held):
            conv, gconv = list(held[0]), list(held[1])
            for lane in range(GROUP):
                m = at * GROUP + lane
                f = row_of(factors, m, t)
                rate = rates[t, pl.ds(m, 1), :]
                res = residues[t, pl.ds(m, 1), :]
                into = edges[m, pl.ds(t, 1), :]
                out = edges[m, pl.ds(tiles + t, 1), :]
                z = res * (enters[m, t] + jnp.exp(-rate * before) * into)
                y = (res * f) * (leaves[m, t] + jnp.exp(-rate * after) * out)
                for i in range(block):
                    conv[i] = conv[i] + z
                    gconv[block - 1 - i] = gconv[block - 1 - i] + y
                    if i < block - 1:
                        z = z * f
                        y = y * f
            return tuple(conv), tuple(gconv)

        start = (
            tuple(convs[t, i] for i in range(block)),
            tuple(gconvs[t, i] for i in range(block)),
        )
        conv, gconv = lax.fori_loop(0, modes // GROUP, body, start)
        for i in range(block):
            mixed[t, pl.ds(i, SUBS, stride=block), :] = conv[i]
            gmix[t, pl.ds(i, SUBS, stride=block), :] = gconv[i]
        whole = mixed[t]
        gwhole = gmix[t]
        gq_ref[:, lanes] = (grad_ref[:, lanes].astype(f32) * whole).astype(jnp.bfloat16)
        gk_ref[:, lanes] = (gwhole * value_ref[:, lanes].astype(f32)).astype(jnp.bfloat16)
        gv_ref[:, lanes] = (gwhole * key_ref[:, lanes].astype(f32)).astype(jnp.bfloat16)

    pl.loop(0, tiles // 2)(finish)

    def owner_total():
        partbox[me] = parts[mode]
        each_peer(lambda d: give(mode, d, d).wait_recv())
        total[...] = jnp.sum(partbox[...], axis=0)
        each_peer(lambda d: spread(d, mode, d).start())
        answer[mode] = total[...]

    if_owner(owner_total)
    pl.loop(tiles // 2, tiles)(finish)
    if_owner(lambda: None, lambda: spread(me, mode, mode * stride).wait_recv())
    each_mode(lambda m: spread(me, m, m * stride).wait_recv())

    squares = jnp.zeros((1, LANES), f32)
    for t in range(tiles):
        lanes = slice(t * LANES, (t + 1) * LANES)
        grad_res = answer[:, t, :] / positions
        grad_rate = (
            -rate_ref[:, lanes] * res_ref[:, lanes] * answer[:, tiles + t, :] / positions
        )
        gres_ref[:, lanes] = grad_res
        grate_ref[:, lanes] = grad_rate
        squares = squares + jnp.sum(
            grad_res * grad_res + grad_rate * grad_rate, axis=0, keepdims=True
        )
    square[0] = jnp.broadcast_to(squares, (SUBS, LANES))

    def partner(p):
        return pltpu.make_async_remote_copy(
            src_ref=square.at[0],
            dst_ref=square.at[p],
            send_sem=send5.at[p],
            recv_sem=recv5.at[p],
            device_id=(me, lax.rem(mine + p, chan)),
            device_id_type=MESH,
        )

    for p in range(1, chan):
        partner(p).start()

    each_mode(lambda m: ask(m, me, m * stride).wait_send())
    each_mode(lambda m: give(m, me, m * stride).wait_send())

    def owner_drain():
        each_peer(lambda d: reply(d, mode, d).wait_send())
        each_peer(lambda d: spread(d, mode, d).wait_send())

    def other_drain():
        ask(mode, me, mode * stride).wait_send()
        give(mode, me, mode * stride).wait_send()

    if_owner(owner_drain, other_drain)

    for p in range(1, chan):
        partner(p).wait()
    everything = jnp.sum(square[...], axis=0)[:1]
    norm_ref[...] = jnp.sqrt(jnp.sum(everything, axis=1, keepdims=True))


def on_device(ctx, chan, query_in, key_in, value_in, grad_out, residue, decay_rate):
    rows, channels = query_in.shape
    modes = residue.shape[0]
    tiles = channels // LANES
    block = rows // SUBS
    f32 = jnp.float32
    vmem = pl.BlockSpec(memory_space=pltpu.VMEM)
    dma = pltpu.SemaphoreType.DMA

    def buffer(*shape):
        return pltpu.VMEM(shape, f32)

    *grads, norm = pl.pallas_call(
        functools.partial(kernel, ctx, chan, rows * ctx),
        in_specs=[vmem] * 6,
        out_specs=[vmem] * 6,
        out_shape=[jax.ShapeDtypeStruct((rows, channels), jnp.bfloat16)] * 3
        + [jax.ShapeDtypeStruct((modes, channels), f32)] * 2
        + [jax.ShapeDtypeStruct((1, 1), f32)],
        scratch_shapes=[
            buffer(tiles, rows, LANES),
            buffer(tiles, rows, LANES),
            buffer(tiles, modes, LANES),
            buffer(tiles, modes, LANES),
            buffer(tiles, modes, LANES),
            buffer(2, modes, LANES),
            buffer(modes, tiles, SUBS, LANES),
            buffer(modes, tiles, SUBS, LANES),
            buffer(tiles, block, SUBS, LANES),
            buffer(tiles, block, SUBS, LANES),
            buffer(modes, 2 * tiles, LANES),
            buffer(modes, 2 * tiles, LANES),
            buffer(modes, tiles, LANES),
            buffer(modes, 2 * tiles, LANES),
            buffer(ctx, 2 * tiles, LANES),
            buffer(ctx, 2 * tiles, LANES),
            buffer(modes, 2 * tiles, LANES),
            buffer(modes, 2 * tiles, LANES),
            buffer(ctx, 2 * tiles, LANES),
            buffer(2 * tiles, LANES),
            buffer(modes, 2 * tiles, LANES),
            buffer(chan, SUBS, LANES),
            dma((modes,)), dma((ctx,)), dma((ctx,)), dma((modes,)),
            dma((modes,)), dma((ctx,)), dma((ctx,)), dma((modes,)),
            dma((chan,)), dma((chan,)),
        ],
        compiler_params=pltpu.CompilerParams(
            collective_id=0, has_side_effects=True, vmem_limit_bytes=24 * 2**20
        ),
        name="hyena",
    )(query_in, key_in, value_in, grad_out, residue, decay_rate)
    return (*grads, norm.reshape(()))


def solution(mesh):
    return jax.shard_map(
        functools.partial(on_device, mesh.shape["ctx"], mesh.shape["chan"]),
        mesh=mesh,
        in_specs=(P("ctx", "chan"),) * 4 + (P(None, "chan"),) * 2,
        out_specs=(P("ctx", "chan"),) * 3 + (P(None, "chan"),) * 2 + (P(),),
        check_vma=False,
    )
```

time: 117 us -> 39.1 us (0.33)
  blocking collectives: 47.7 us -> 0 us
  Pallas kernels: 0 us -> 27.9 us
  waiting for transfers between devices: 14 us -> 0 us
  matrix products: 12.7 us -> 0 us
  starting transfers between devices: 11.5 us -> 0 us
  other arithmetic: 11.3 us -> 0 us
  local copies, waits for them, and re-layouts: 16.4 us -> 8.32 us
    all_gather x2 -> x0, blocking collectives: 42.2 us -> none  [the longest x1 23.2 us: on_device(): lax.all_gather(res_sum, 'ctx', axis=1, tiled=True)]
    pallas_call x0 -> x1, Pallas kernels: none -> 27.9 us  [on_device(): pl.pallas_call(functools.partial(kernel, ctx, chan, rows * ctx), in_specs...]
    all_to_all x2 -> x0, waiting for transfers between devices: 14 us -> none  [the longest x1 14 us: on_device(): lax.all_to_all(stacked, 'ctx', split_axis=2, concat_axis=2, tiled=True)]
    dot_general x3 -> x0, matrix products: 12.7 us -> none  [tri_product(): jnp.dot(matrix, flat, preferred_element_type=jnp.float32, precision=lax.P...]
    all_to_all x2 -> x0, starting transfers between devices: 11.5 us -> none  [the longest x1 7.39 us: on_device(): lax.all_to_all(stacked, 'ctx', split_axis=2, concat_axis=2, tiled=True)]
    reduce_sum x4 -> x0, other arithmetic: 8.14 us -> none  [the longest x1 6.86 us: sweep(): res_sum = jnp.sum(mixed_in[:, None, :] * adjoint, axis=0)]
    psum x1 -> x0, blocking collectives: 5.55 us -> none  [on_device(): filter_norm = jnp.sqrt(lax.psum(squares, 'chan'))]
    unnamed x30 -> x17, local copies, waits for them, and re-layouts: 10.9 us -> 8.32 us
  transfers between devices with their start and end apart: 2 -> 0, of which waited for: 1 -> 0; matrix products, arithmetic and copies ran while one was open for 2% -> 0% of each run, Pallas kernels for 0% -> 0%
where the time goes in v2:
time: 39.1 us; the launch traced here: 38.7 us
  Pallas kernels  27.9 us (71%)
  local copies, waits for them, and re-layouts  8.32 us (21%)
  between operations  2.48 us (6%)
    pallas_call x1, Pallas kernels, on_device(): pl.pallas_call(functools.partial(kernel, ctx, chan, rows * ctx), in_specs...  27.9 us
    unnamed x17, local copies, waits for them, and re-layouts  8.32 us

profile of v2, /device:TPU:0, one launch (start us, length us, event | category | flops | bytes accessed | tf_op | source)
XLA Modules:
  0.0 38.7 jit_solution(10015623016988680113)
XLA Ops:
  0.6 0.0 copy-start
  0.6 0.9 %copy-done = bf16[128,512]{1,0:T(8,128)(2,1)S(1)} copy-done((bf16[128,512]{1,0:T(8,128)(2,1)S(1)}, bf16[128,512]{1,0:T(8,128)(2,1)}, u32[]{:S(2)}) %copy-start) | copy-done | bytes 131096
  1.5 0.0 copy-start.1
  1.5 0.9 %copy-done.1 = bf16[128,512]{1,0:T(8,128)(2,1)S(1)} copy-done((bf16[128,512]{1,0:T(8,128)(2,1)S(1)}, bf16[128,512]{1,0:T(8,128)(2,1)}, u32[]{:S(2)}) %copy-start.1) | copy-done | bytes 131096
  2.4 0.0 copy-start.2
  2.4 0.9 %copy-done.2 = bf16[128,512]{1,0:T(8,128)(2,1)S(1)} copy-done((bf16[128,512]{1,0:T(8,128)(2,1)S(1)}, bf16[128,512]{1,0:T(8,128)(2,1)}, u32[]{:S(2)}) %copy-start.2) | copy-done | bytes 131096
  3.3 0.0 copy-start.3
  3.4 0.9 %copy-done.3 = bf16[128,512]{1,0:T(8,128)(2,1)S(1)} copy-done((bf16[128,512]{1,0:T(8,128)(2,1)S(1)}, bf16[128,512]{1,0:T(8,128)(2,1)}, u32[]{:S(2)}) %copy-start.3) | copy-done | bytes 131096
  4.3 0.0 copy-start.4
  4.3 0.8 %copy-done.4 = f32[16,512]{1,0:T(8,128)S(1)} copy-done((f32[16,512]{1,0:T(8,128)S(1)}, f32[16,512]{1,0:T(8,128)}, u32[]{:S(2)}) %copy-start.4) | copy-done | bytes 32792
  5.0 0.0 copy-start.5
  5.0 0.8 %copy-done.5 = f32[16,512]{1,0:T(8,128)S(1)} copy-done((f32[16,512]{1,0:T(8,128)S(1)}, f32[16,512]{1,0:T(8,128)}, u32[]{:S(2)}) %copy-start.5) | copy-done | bytes 32792
  5.8 27.9 %hyena.1 = (bf16[128,512]{1,0:T(8,128)(2,1)S(1)}, bf16[128,512]{1,0:T(8,128)(2,1)S(1)}, bf16[128,512]{1,0:T(8,128)(2,1)S(1)}, f32[16,512]{1,0:T(8,128)S(1)}, f32[16,512]{1,0:T(8,128)S(1)}, /*index=5*/f32[1,1]{1,0:T(1,128)}) custom-call(bf16[128,512]{1,0:T(8,128)(2,1)S(1)} %copy-done, bf16[128,512]{1,0:T(8,128)(2,1)S(1)} %copy-done.1, ...), custom_call_target="tpu_custom_call" | custom-call | tf_op jit(solution)/shard_map/hyena/pallas_call | solution.py:347
  33.7 0.7 %copy.18 = bf16[128,512]{1,0:T(8,128)(2,1)} copy(bf16[128,512]{1,0:T(8,128)(2,1)S(1)} %get-tuple-element.24) | data formatting | bytes 262144
  34.4 0.7 %copy.19 = bf16[128,512]{1,0:T(8,128)(2,1)} copy(bf16[128,512]{1,0:T(8,128)(2,1)S(1)} %get-tuple-element.25) | data formatting | bytes 262144
  35.0 0.7 %copy.20 = bf16[128,512]{1,0:T(8,128)(2,1)} copy(bf16[128,512]{1,0:T(8,128)(2,1)S(1)} %get-tuple-element.26) | data formatting | bytes 262144
  35.7 0.6 %copy.21 = f32[16,512]{1,0:T(8,128)} copy(f32[16,512]{1,0:T(8,128)S(1)} %get-tuple-element.27) | data formatting | bytes 65536
  36.3 0.6 %copy.22 = f32[16,512]{1,0:T(8,128)} copy(f32[16,512]{1,0:T(8,128)S(1)} %get-tuple-element.28) | data formatting | bytes 65536
Async XLA Ops:
  0.6 0.9 %copy-start = (bf16[128,512]{1,0:T(8,128)(2,1)S(1)}, bf16[128,512]{1,0:T(8,128)(2,1)}, u32[]{:S(2)}) copy-start(bf16[128,512]{1,0:T(8,128)(2,1)} %query_ref.1) | copy-start | bytes 393220
  1.5 0.9 %copy-start.1 = (bf16[128,512]{1,0:T(8,128)(2,1)S(1)}, bf16[128,512]{1,0:T(8,128)(2,1)}, u32[]{:S(2)}) copy-start(bf16[128,512]{1,0:T(8,128)(2,1)} %key_ref.1) | copy-start | bytes 393220
  2.4 0.9 %copy-start.2 = (bf16[128,512]{1,0:T(8,128)(2,1)S(1)}, bf16[128,512]{1,0:T(8,128)(2,1)}, u32[]{:S(2)}) copy-start(bf16[128,512]{1,0:T(8,128)(2,1)} %value_ref.1) | copy-start | bytes 393220
  3.3 0.9 %copy-start.3 = (bf16[128,512]{1,0:T(8,128)(2,1)S(1)}, bf16[128,512]{1,0:T(8,128)(2,1)}, u32[]{:S(2)}) copy-start(bf16[128,512]{1,0:T(8,128)(2,1)} %grad_ref.1) | copy-start | bytes 393220
  4.3 0.8 %copy-start.4 = (f32[16,512]{1,0:T(8,128)S(1)}, f32[16,512]{1,0:T(8,128)}, u32[]{:S(2)}) copy-start(f32[16,512]{1,0:T(8,128)} %res_ref.1) | copy-start | bytes 98308
  5.0 0.8 %copy-start.5 = (f32[16,512]{1,0:T(8,128)S(1)}, f32[16,512]{1,0:T(8,128)}, u32[]{:S(2)}) copy-start(f32[16,512]{1,0:T(8,128)} %rate_ref.1) | copy-start | bytes 98308

commit v3 on v2

v3 whole, which is shorter than its diff:
```python
import functools

import jax
import jax.numpy as jnp
from jax import lax
from jax.experimental import pallas as pl
from jax.experimental.pallas import tpu as pltpu
from jax.sharding import PartitionSpec as P

MESH = pl.DeviceIdType.MESH
LANES = 128
SUBS = 8
GROUP = 4


def kernel(
    ctx, chan, positions,
    query_ref, key_ref, value_ref, grad_ref, res_ref, rate_ref,
    gq_ref, gk_ref, gv_ref, gres_ref, grate_ref, norm_ref,
    mixed, gmix, factors, rates, residues, lags, enters, leaves, convs, gconvs, spans,
    sums, twin, chipsum, inbox, outbox, halfedge, twinedge, edges, total, answer, square,
    send0, recv0, send1, recv1, send2, recv2, send3, recv3, send4, recv4, send5, recv5,
):
    modes, channels = res_ref.shape
    tiles = channels // LANES
    rows = query_ref.shape[0]
    block = rows // SUBS
    chips = ctx // 2
    half = modes // 2
    stride = chips // half
    me = lax.axis_index("ctx")
    mine = lax.axis_index("chan")
    chip = me // 2
    core = lax.rem(me, 2)
    sibling = 2 * chip + 1 - core
    owned = chip // stride
    mode = core * half + owned
    own_half = pl.ds(core * half, half)
    other_half = pl.ds((1 - core) * half, half)
    f32 = jnp.float32

    barrier = pltpu.get_barrier_semaphore()

    @pl.loop(1, ctx)
    def _(p):
        pl.semaphore_signal(
            barrier, inc=1, device_id=(lax.rem(me + p, ctx), mine), device_id_type=MESH
        )

    for p in range(1, chan):
        pl.semaphore_signal(
            barrier, inc=1, device_id=(me, lax.rem(mine + p, chan)), device_id_type=MESH
        )

    sub = lax.broadcasted_iota(jnp.int32, (SUBS, LANES), 0)
    before = sub.astype(f32) * float(block)
    after = (SUBS - 1 - sub).astype(f32) * float(block)

    def lanes_of(t):
        return pl.ds(pl.multiple_of(t * LANES, LANES), LANES)

    def blocks_of(ref, t):
        return [ref[t, pl.ds(i, SUBS, stride=block), :] for i in range(block)]

    def row_of(ref, m, t):
        return jnp.broadcast_to(ref[t, pl.ds(m, 1), :], (SUBS, LANES))

    @pl.loop(0, tiles)
    def _(t):
        lanes = lanes_of(t)
        mixed[t] = key_ref[:, lanes].astype(f32) * value_ref[:, lanes].astype(f32)
        gmix[t] = grad_ref[:, lanes].astype(f32) * query_ref[:, lanes].astype(f32)
        rates[t] = rate_ref[:, lanes]
        residues[t] = res_ref[:, lanes]
        factors[t] = jnp.exp(-rates[t])
        x = blocks_of(mixed, t)
        g = blocks_of(gmix, t)
        factor = factors[t]
        res = residues[t]
        power = jnp.ones_like(factor)
        taps = []
        lag_res = jnp.zeros_like(factor)
        lag_rate = jnp.zeros_like(factor)
        for j in range(block):
            tap = jnp.sum(res * power, axis=0, keepdims=True)
            taps.append(jnp.broadcast_to(tap, (SUBS, LANES)))
            products = x[0] * g[j]
            for i in range(1, block - j):
                products = products + x[i] * g[i + j]
            term = power * jnp.sum(products, axis=0, keepdims=True)
            lag_res = lag_res + term
            lag_rate = lag_rate + float(j) * term
            power = power * factor
        for i in range(block):
            acc = taps[0] * x[i]
            for j in range(1, i + 1):
                acc = acc + taps[j] * x[i - j]
            convs[t, i] = acc
            acc = taps[0] * g[i]
            for j in range(1, block - i):
                acc = acc + taps[j] * g[i + j]
            gconvs[t, i] = acc
        lags[0] = lag_res
        lags[1] = lag_rate

        @pl.loop(0, modes // GROUP)
        def _(at):
            for lane in range(GROUP):
                m = at * GROUP + lane
                f = row_of(factors, m, t)
                head = x[0] * f
                head1 = head
                tail = g[block - 1]
                tail1 = jnp.zeros_like(tail)
                for i in range(1, block):
                    head = (head + x[i]) * f
                    head1 = head1 * f + head
                    tail1 = (tail1 + tail) * f
                    tail = tail * f + g[block - 1 - i]
                rate = rates[t, pl.ds(m, 1), :]
                step = jnp.exp(rate * -float(block))
                up, down, weight = head, tail, jnp.broadcast_to(step, (SUBS, LANES))
                for shift in (1, 2, 4):
                    up = up + jnp.where(sub >= shift, weight * pltpu.roll(up, shift, 0), 0.0)
                    down = down + jnp.where(
                        sub < SUBS - shift, weight * pltpu.roll(down, SUBS - shift, 0), 0.0
                    )
                    weight = weight * weight
                enter = jnp.where(sub >= 1, pltpu.roll(up, 1, 0), 0.0)
                leave = jnp.where(sub < SUBS - 1, pltpu.roll(down, SUBS - 1, 0), 0.0)
                enters[m, t] = enter
                leaves[m, t] = leave
                moment = jnp.exp(-rate * after) * (head1 + after * head)
                gmoment = jnp.exp(-rate * before) * (tail1 + before * tail)
                cross = head * leave
                cross1 = head1 * leave + enter * (tail1 + float(block) * step * leave)
                found = (
                    up[SUBS - 1 :],
                    down[:1],
                    jnp.sum(moment, axis=0, keepdims=True),
                    jnp.sum(gmoment, axis=0, keepdims=True),
                    jnp.sum(cross, axis=0, keepdims=True) + lags[0, pl.ds(m, 1), :],
                    jnp.sum(cross1, axis=0, keepdims=True) + lags[1, pl.ds(m, 1), :],
                )
                for at_row, row in enumerate(found):
                    sums[m, pl.ds(at_row * tiles + t, 1), :] = row
                spans[m, pl.ds(t, 1), :] = weight[:1]

    pl.semaphore_wait(barrier, ctx - 1 + chan - 1)

    def remote(src, dst, send, recv, target):
        return pltpu.make_async_remote_copy(
            src_ref=src, dst_ref=dst, send_sem=send, recv_sem=recv,
            device_id=(target, mine), device_id_type=MESH,
        )

    def pair_up():
        return remote(sums.at[other_half], twin, send0, recv0, sibling)

    def ask(j, slot, at):
        return remote(
            chipsum.at[j], inbox.at[slot], send1.at[j], recv1.at[slot], 2 * at + core
        )

    def reply(h, slot):
        return remote(
            outbox.at[h], halfedge.at[slot], send2.at[h], recv2.at[slot], 2 * h + core
        )

    def pair_down():
        return remote(twinedge, edges.at[own_half], send3, recv3, sibling)

    def spread(d, slot):
        return remote(total, answer.at[slot], send4.at[d], recv4.at[slot], d)

    def if_owner(then, otherwise=None):
        if stride == 1:
            then()
            return
        owner = lax.rem(chip, stride) == 0
        pl.when(owner)(then)
        if otherwise is not None:
            pl.when(jnp.logical_not(owner))(otherwise)

    def each(count, start, act):
        @pl.loop(1, count)
        def _(p):
            act(lax.rem(start + p, count))

    def part(ref, k):
        return ref[:, k * tiles : (k + 1) * tiles, :]

    pair_up().start()
    pair_up().wait_recv()
    first = core == 0
    span = spans[own_half]

    def ordered(k):
        here = sums[own_half, k * tiles : (k + 1) * tiles, :]
        there = part(twin, k)
        return jnp.where(first, here, there), jnp.where(first, there, here)

    (xa, xb), (ga, gb), (ma, mb), (na, nb), (ra, rb), (qa, qb) = [ordered(k) for k in range(6)]
    joined = (
        span * xa + xb,
        ga + span * gb,
        span * (ma + float(rows) * xa) + mb,
        na + span * (nb + float(rows) * gb),
        ra + rb + xa * gb,
        qa + qb + ma * gb + xa * nb,
    )
    for k, found in enumerate(joined):
        chipsum[:, k * tiles : (k + 1) * tiles, :] = found

    each(half, owned, lambda j: ask(j, chip, j * stride).start())
    if_owner(lambda: None, lambda: ask(owned, chip, owned * stride).start())

    def owner_prefix():
        inbox[chip] = chipsum[owned]
        each(chips, chip, lambda h: ask(owned, h, h).wait_recv())
        span2 = spans[mode] * spans[mode]
        enter = jnp.zeros_like(span2)
        leave = jnp.zeros_like(span2)
        for h in range(chips):
            outbox[h, 0:tiles, :] = enter
            enter = span2 * enter + inbox[h, 0:tiles, :]
            back = chips - 1 - h
            outbox[back, tiles : 2 * tiles, :] = leave
            leave = span2 * leave + inbox[back, tiles : 2 * tiles, :]
        each(chips, chip, lambda h: reply(h, owned).start())
        halfedge[owned] = outbox[chip]
        enter = part(outbox, 0)
        leave = part(outbox, 1)
        res_total = part(inbox, 4) + part(inbox, 0) * leave
        rate_total = (
            part(inbox, 5)
            + part(inbox, 2) * leave
            + enter * (part(inbox, 3) + float(2 * rows) * span2 * leave)
        )
        total[0:tiles, :] = jnp.sum(res_total, axis=0)
        total[tiles : 2 * tiles, :] = jnp.sum(rate_total, axis=0)
        each(ctx, me, lambda d: spread(d, mode).start())
        answer[mode] = total[...]

    if_owner(owner_prefix, lambda: reply(chip, owned).wait_recv())
    each(half, owned, lambda j: reply(chip, j).wait_recv())

    enter = part(halfedge, 0)
    leave = part(halfedge, 1)
    enter_b = span * enter + xa
    leave_a = span * leave + gb
    edges[own_half, 0:tiles, :] = jnp.where(first, enter, enter_b)
    edges[own_half, tiles : 2 * tiles, :] = jnp.where(first, leave_a, leave)
    twinedge[:, 0:tiles, :] = jnp.where(first, enter_b, enter)
    twinedge[:, tiles : 2 * tiles, :] = jnp.where(first, leave, leave_a)
    pair_down().start()
    pair_down().wait_recv()

    def finish(t):
        lanes = lanes_of(t)

        def body(at, held):
            conv, gconv = list(held[0]), list(held[1])
            for lane in range(GROUP):
                m = at * GROUP + lane
                f = row_of(factors, m, t)
                rate = rates[t, pl.ds(m, 1), :]
                res = residues[t, pl.ds(m, 1), :]
                into = edges[m, pl.ds(t, 1), :]
                out = edges[m, pl.ds(tiles + t, 1), :]
                z = res * (enters[m, t] + jnp.exp(-rate * before) * into)
                y = (res * f) * (leaves[m, t] + jnp.exp(-rate * after) * out)
                for i in range(block):
                    conv[i] = conv[i] + z
                    gconv[block - 1 - i] = gconv[block - 1 - i] + y
                    if i < block - 1:
                        z = z * f
                        y = y * f
            return tuple(conv), tuple(gconv)

        start = (
            tuple(convs[t, i] for i in range(block)),
            tuple(gconvs[t, i] for i in range(block)),
        )
        conv, gconv = lax.fori_loop(0, modes // GROUP, body, start)
        for i in range(block):
            mixed[t, pl.ds(i, SUBS, stride=block), :] = conv[i]
            gmix[t, pl.ds(i, SUBS, stride=block), :] = gconv[i]
        whole = mixed[t]
        gwhole = gmix[t]
        gq_ref[:, lanes] = (grad_ref[:, lanes].astype(f32) * whole).astype(jnp.bfloat16)
        gk_ref[:, lanes] = (gwhole * value_ref[:, lanes].astype(f32)).astype(jnp.bfloat16)
        gv_ref[:, lanes] = (gwhole * key_ref[:, lanes].astype(f32)).astype(jnp.bfloat16)

    pl.loop(0, tiles // 2)(finish)

    if_owner(lambda: None, lambda: spread(me, mode).wait_recv())
    each(modes, mode, lambda m: spread(me, m).wait_recv())

    squares = jnp.zeros((1, LANES), f32)
    for t in range(tiles):
        lanes = slice(t * LANES, (t + 1) * LANES)
        grad_res = answer[:, t, :] / positions
        grad_rate = (
            -rate_ref[:, lanes] * res_ref[:, lanes] * answer[:, tiles + t, :] / positions
        )
        gres_ref[:, lanes] = grad_res
        grate_ref[:, lanes] = grad_rate
        squares = squares + jnp.sum(
            grad_res * grad_res + grad_rate * grad_rate, axis=0, keepdims=True
        )
    square[0] = jnp.broadcast_to(squares, (SUBS, LANES))

    def partner(p):
        return pltpu.make_async_remote_copy(
            src_ref=square.at[0],
            dst_ref=square.at[p],
            send_sem=send5.at[p],
            recv_sem=recv5.at[p],
            device_id=(me, lax.rem(mine + p, chan)),
            device_id_type=MESH,
        )

    for p in range(1, chan):
        partner(p).start()

    pl.loop(tiles // 2, tiles)(finish)

    pair_up().wait_send()
    pair_down().wait_send()
    each(half, owned, lambda j: ask(j, chip, j * stride).wait_send())

    def owner_drain():
        each(chips, chip, lambda h: reply(h, owned).wait_send())
        each(ctx, me, lambda d: spread(d, mode).wait_send())

    if_owner(owner_drain, lambda: ask(owned, chip, owned * stride).wait_send())

    for p in range(1, chan):
        partner(p).wait()
    everything = jnp.sum(square[...], axis=0)[:1]
    norm_ref[...] = jnp.sqrt(jnp.sum(everything, axis=1, keepdims=True))


def copy_kernel(*refs):
    count = len(refs) // 2
    sems = refs[-1]
    copies = [
        pltpu.make_async_copy(refs[i], refs[count + i], sems.at[i]) for i in range(count)
    ]
    for copy in copies:
        copy.start()
    for copy in copies:
        copy.wait()


def on_device(ctx, chan, query_in, key_in, value_in, grad_out, residue, decay_rate):
    rows, channels = query_in.shape
    modes = residue.shape[0]
    tiles = channels // LANES
    block = rows // SUBS
    chips = ctx // 2
    half = modes // 2
    f32 = jnp.float32
    vmem = pl.BlockSpec(memory_space=pltpu.VMEM)
    dma = pltpu.SemaphoreType.DMA

    def buffer(*shape):
        return pltpu.VMEM(shape, f32)

    shapes = (
        [jax.ShapeDtypeStruct((rows, channels), jnp.bfloat16)] * 3
        + [jax.ShapeDtypeStruct((modes, channels), f32)] * 2
        + [jax.ShapeDtypeStruct((1, 1), f32)]
    )
    found = pl.pallas_call(
        functools.partial(kernel, ctx, chan, rows * ctx),
        in_specs=[vmem] * 6,
        out_specs=[vmem] * 6,
        out_shape=shapes,
        scratch_shapes=[
            buffer(tiles, rows, LANES),
            buffer(tiles, rows, LANES),
            buffer(tiles, modes, LANES),
            buffer(tiles, modes, LANES),
            buffer(tiles, modes, LANES),
            buffer(2, modes, LANES),
            buffer(modes, tiles, SUBS, LANES),
            buffer(modes, tiles, SUBS, LANES),
            buffer(tiles, block, SUBS, LANES),
            buffer(tiles, block, SUBS, LANES),
            buffer(modes, tiles, LANES),
            buffer(modes, 6 * tiles, LANES),
            buffer(half, 6 * tiles, LANES),
            buffer(half, 6 * tiles, LANES),
            buffer(chips, 6 * tiles, LANES),
            buffer(chips, 2 * tiles, LANES),
            buffer(half, 2 * tiles, LANES),
            buffer(half, 2 * tiles, LANES),
            buffer(modes, 2 * tiles, LANES),
            buffer(2 * tiles, LANES),
            buffer(modes, 2 * tiles, LANES),
            buffer(chan, SUBS, LANES),
            dma, dma, dma((half,)), dma((chips,)), dma((chips,)), dma((half,)),
            dma, dma, dma((ctx,)), dma((modes,)), dma((chan,)), dma((chan,)),
        ],
        compiler_params=pltpu.CompilerParams(collective_id=0, has_side_effects=True),
        name="hyena",
    )(query_in, key_in, value_in, grad_out, residue, decay_rate)
    anywhere = pl.BlockSpec(memory_space=pl.ANY)
    *grads, norm = pl.pallas_call(
        copy_kernel,
        in_specs=[anywhere] * len(shapes),
        out_specs=[anywhere] * len(shapes),
        out_shape=shapes,
        scratch_shapes=[dma((len(shapes),))],
        name="place",
    )(*found)
    return (*grads, norm.reshape(()))


def solution(mesh):
    return jax.shard_map(
        functools.partial(on_device, mesh.shape["ctx"], mesh.shape["chan"]),
        mesh=mesh,
        in_specs=(P("ctx", "chan"),) * 4 + (P(None, "chan"),) * 2,
        out_specs=(P("ctx", "chan"),) * 3 + (P(None, "chan"),) * 2 + (P(),),
        check_vma=False,
    )
```

time: 39.1 us -> 39 us (level)
  Pallas kernels: 27.9 us -> 38.2 us
  local copies, waits for them, and re-layouts: 8.32 us -> 0 us
  between operations: 2.48 us -> 0.64 us
    pallas_call x0 -> x1, Pallas kernels: none -> 15.7 us  [on_device(): pl.pallas_call(copy_kernel, in_specs=[anywhere] * len(shapes), out_specs=...]
    unnamed x17 -> x0, local copies, waits for them, and re-layouts: 8.32 us -> none
    pallas_call x1, Pallas kernels: 27.9 us -> 22.5 us  [on_device(): pl.pallas_call(functools.partial(kernel, ctx, chan, rows * ctx), in_specs...]
where the time goes in v3:
time: 39 us; the launch traced here: 38.9 us
  Pallas kernels  38.2 us (98%)
  between operations  0.64 us (2%)
    pallas_call x1, Pallas kernels, on_device(): pl.pallas_call(functools.partial(kernel, ctx, chan, rows * ctx), in_specs...  22.5 us
    pallas_call x1, Pallas kernels, on_device(): pl.pallas_call(copy_kernel, in_specs=[anywhere] * len(shapes), out_specs=...  15.7 us

profile of v3, /device:TPU:0, one launch (start us, length us, event | category | flops | bytes accessed | tf_op | source)
XLA Modules:
  0.0 38.9 jit_solution(6289839921966856278)
XLA Ops:
  0.6 22.5 %hyena.1 = (bf16[128,512]{1,0:T(8,128)(2,1)}, bf16[128,512]{1,0:T(8,128)(2,1)}, bf16[128,512]{1,0:T(8,128)(2,1)}, f32[16,512]{1,0:T(8,128)}, f32[16,512]{1,0:T(8,128)}, /*index=5*/f32[1,1]{1,0:T(1,128)}) custom-call(bf16[128,512]{1,0:T(8,128)(2,1)} %query_ref.1, bf16[128,512]{1,0:T(8,128)(2,1)} %key_ref.1, bf16[128,512]{1,0:T(8,128)(2,1)} %value_ref.1, ...), custom_call_target="tpu_custom_call" | custom-call | tf_op jit(solution)/shard_map/hyena/pallas_call | solution.py:376
  23.2 15.7 %place.1 = (bf16[128,512]{1,0:T(8,128)(2,1)}, bf16[128,512]{1,0:T(8,128)(2,1)}, bf16[128,512]{1,0:T(8,128)(2,1)}, f32[16,512]{1,0:T(8,128)}, f32[16,512]{1,0:T(8,128)}, /*index=5*/f32[1,1]{1,0:T(1,128)}) custom-call(bf16[128,512]{1,0:T(8,128)(2,1)} %get-tuple-element.18.refs_0_, bf16[128,512]{1,0:T(8,128)(2,1)} %get-tuple-element.19.refs_1_, ...), custom_call_target="tpu_custom_call" | custom-call | tf_op jit(solution)/shard_map/place/pallas_call | solution.py:411

commit v4 on v3

--- a/solution.py
+++ b/solution.py
@@ -18,8 +18,9 @@
     query_ref, key_ref, value_ref, grad_ref, res_ref, rate_ref,
     gq_ref, gk_ref, gv_ref, gres_ref, grate_ref, norm_ref,
     mixed, gmix, factors, rates, residues, lags, enters, leaves, convs, gconvs, spans,
-    sums, twin, chipsum, inbox, outbox, halfedge, twinedge, edges, total, answer, square,
+    sums, sums2, twin, twin2, chipsum, chipsum2, inbox, inbox2, outbox, halfedge, twinedge, edges, total, answer, square,
     send0, recv0, send1, recv1, send2, recv2, send3, recv3, send4, recv4, send5, recv5,
+    send6, recv6, send7, recv7,
 ):
     modes, channels = res_ref.shape
     tiles = channels // LANES
@@ -73,6 +74,90 @@
         rates[t] = rate_ref[:, lanes]
         residues[t] = res_ref[:, lanes]
         factors[t] = jnp.exp(-rates[t])
+        x = blocks_of(mixed, t)
+        g = blocks_of(gmix, t)
+
+        @pl.loop(0, modes // GROUP)
+        def _(at):
+            for lane in range(GROUP):
+                m = at * GROUP + lane
+                f = row_of(factors, m, t)
+                head = x[0] * f
+                tail = g[block - 1]
+                for i in range(1, block):
+                    head = (head + x[i]) * f
+                    tail = tail * f + g[block - 1 - i]
+                weight = jnp.exp(rates[t, pl.ds(m, 1), :] * -float(block))
+                weight = jnp.broadcast_to(weight, (SUBS, LANES))
+                up, down = head, tail
+                for shift in (1, 2, 4):
+                    up = up + jnp.where(sub >= shift, weight * pltpu.roll(up, shift, 0), 0.0)
+                    down = down + jnp.where(
+                        sub < SUBS - shift, weight * pltpu.roll(down, SUBS - shift, 0), 0.0
+                    )
+                    weight = weight * weight
+                enters[m, t] = jnp.where(sub >= 1, pltpu.roll(up, 1, 0), 0.0)
+                leaves[m, t] = jnp.where(sub < SUBS - 1, pltpu.roll(down, SUBS - 1, 0), 0.0)
+                sums[m, pl.ds(t, 1), :] = up[SUBS - 1 :]
+                sums[m, pl.ds(tiles + t, 1), :] = down[:1]
+                spans[m, pl.ds(t, 1), :] = weight[:1]
+
+    pl.semaphore_wait(barrier, ctx - 1 + chan - 1)
+
+    def remote(src, dst, send, recv, target):
+        return pltpu.make_async_remote_copy(
+            src_ref=src, dst_ref=dst, send_sem=send, recv_sem=recv,
+            device_id=(target, mine), device_id_type=MESH,
+        )
+
+    def pair_up():
+        return remote(sums.at[other_half], twin, send0, recv0, sibling)
+
+    def pair_up2():
+        return remote(sums2.at[other_half], twin2, send6, recv6, sibling)
+
+    def ask(j, slot, at):
+        return remote(
+            chipsum.at[j], inbox.at[slot], send1.at[j], recv1.at[slot], 2 * at + core
+        )
+
+    def ask2(j, slot, at):
+        return remote(
+            chipsum2.at[j], inbox2.at[slot], send7.at[j], recv7.at[slot], 2 * at + core
+        )
+
+    def reply(h, slot):
+        return remote(
+            outbox.at[h], halfedge.at[slot], send2.at[h], recv2.at[slot], 2 * h + core
+        )
+
+    def pair_down():
+        return remote(twinedge, edges.at[own_half], send3, recv3, sibling)
+
+    def spread(d, slot):
+        return remote(total, answer.at[slot], send4.at[d], recv4.at[slot], d)
+
+    def if_owner(then, otherwise=None):
+        if stride == 1:
+            then()
+            return
+        owner = lax.rem(chip, stride) == 0
+        pl.when(owner)(then)
+        if otherwise is not None:
+            pl.when(jnp.logical_not(owner))(otherwise)
+
+    def each(count, start, act):
+        @pl.loop(1, count)
+        def _(p):
+            act(lax.rem(start + p, count))
+
+    def part(ref, k):
+        return ref[:, k * tiles : (k + 1) * tiles, :]
+
+    pair_up().start()
+
+    @pl.loop(0, tiles)
+    def _(t):
         x = blocks_of(mixed, t)
         g = blocks_of(gmix, t)
         factor = factors[t]
@@ -100,8 +185,28 @@
             for j in range(1, block - i):
                 acc = acc + taps[j] * g[i + j]
             gconvs[t, i] = acc
-        lags[0] = lag_res
-        lags[1] = lag_rate
+        lags[0, t] = lag_res
+        lags[1, t] = lag_rate
+
+    first = core == 0
+    span = spans[own_half]
+
+    def ordered(mine_ref, twin_ref, k):
+        here = mine_ref[own_half, k * tiles : (k + 1) * tiles, :]
+        there = part(twin_ref, k)
+        return jnp.where(first, here, there), jnp.where(first, there, here)
+
+    pair_up().wait_recv()
+    (xa, xb), (ga, gb) = [ordered(sums, twin, k) for k in range(2)]
+    chipsum[:, 0:tiles, :] = span * xa + xb
+    chipsum[:, tiles : 2 * tiles, :] = ga + span * gb
+    each(half, owned, lambda j: ask(j, chip, j * stride).start())
+    if_owner(lambda: None, lambda: ask(owned, chip, owned * stride).start())
+
+    @pl.loop(0, tiles)
+    def _(t):
+        x = blocks_of(mixed, t)
+        g = blocks_of(gmix, t)
 
         @pl.loop(0, modes // GROUP)
         def _(at):
@@ -119,101 +224,22 @@
                     tail = tail * f + g[block - 1 - i]
                 rate = rates[t, pl.ds(m, 1), :]
                 step = jnp.exp(rate * -float(block))
-                up, down, weight = head, tail, jnp.broadcast_to(step, (SUBS, LANES))
-                for shift in (1, 2, 4):
-                    up = up + jnp.where(sub >= shift, weight * pltpu.roll(up, shift, 0), 0.0)
-                    down = down + jnp.where(
-                        sub < SUBS - shift, weight * pltpu.roll(down, SUBS - shift, 0), 0.0
-                    )
-                    weight = weight * weight
-                enter = jnp.where(sub >= 1, pltpu.roll(up, 1, 0), 0.0)
-                leave = jnp.where(sub < SUBS - 1, pltpu.roll(down, SUBS - 1, 0), 0.0)
-                enters[m, t] = enter
-                leaves[m, t] = leave
+                enter = enters[m, t]
+                leave = leaves[m, t]
                 moment = jnp.exp(-rate * after) * (head1 + after * head)
                 gmoment = jnp.exp(-rate * before) * (tail1 + before * tail)
                 cross = head * leave
                 cross1 = head1 * leave + enter * (tail1 + float(block) * step * leave)
                 found = (
-                    up[SUBS - 1 :],
-                    down[:1],
                     jnp.sum(moment, axis=0, keepdims=True),
                     jnp.sum(gmoment, axis=0, keepdims=True),
-                    jnp.sum(cross, axis=0, keepdims=True) + lags[0, pl.ds(m, 1), :],
-                    jnp.sum(cross1, axis=0, keepdims=True) + lags[1, pl.ds(m, 1), :],
+                    jnp.sum(cross, axis=0, keepdims=True) + lags[0, t, pl.ds(m, 1), :],
+                    jnp.sum(cross1, axis=0, keepdims=True) + lags[1, t, pl.ds(m, 1), :],
                 )
                 for at_row, row in enumerate(found):
-                    sums[m, pl.ds(at_row * tiles + t, 1), :] = row
-                spans[m, pl.ds(t, 1), :] = weight[:1]
-
-    pl.semaphore_wait(barrier, ctx - 1 + chan - 1)
-
-    def remote(src, dst, send, recv, target):
-        return pltpu.make_async_remote_copy(
-            src_ref=src, dst_ref=dst, send_sem=send, recv_sem=recv,
-            device_id=(target, mine), device_id_type=MESH,
-        )
-
-    def pair_up():
-        return remote(sums.at[other_half], twin, send0, recv0, sibling)
-
-    def ask(j, slot, at):
-        return remote(
-            chipsum.at[j], inbox.at[slot], send1.at[j], recv1.at[slot], 2 * at + core
-        )
-
-    def reply(h, slot):
-        return remote(
-            outbox.at[h], halfedge.at[slot], send2.at[h], recv2.at[slot], 2 * h + core
-        )
-
-    def pair_down():
-        return remote(twinedge, edges.at[own_half], send3, recv3, sibling)
-
-    def spread(d, slot):
-        return remote(total, answer.at[slot], send4.at[d], recv4.at[slot], d)
-
-    def if_owner(then, otherwise=None):
-        if stride == 1:
-            then()
-            return
-        owner = lax.rem(chip, stride) == 0
-        pl.when(owner)(then)
-        if otherwise is not None:
-            pl.when(jnp.logical_not(owner))(otherwise)
-
-    def each(count, start, act):
-        @pl.loop(1, count)
-        def _(p):
-            act(lax.rem(start + p, count))
-
-    def part(ref, k):
-        return ref[:, k * tiles : (k + 1) * tiles, :]
-
-    pair_up().start()
-    pair_up().wait_recv()
-    first = core == 0
-    span = spans[own_half]
-
-    def ordered(k):
-        here = sums[own_half, k * tiles : (k + 1) * tiles, :]
-        there = part(twin, k)
-        return jnp.where(first, here, there), jnp.where(first, there, here)
-
-    (xa, xb), (ga, gb), (ma, mb), (na, nb), (ra, rb), (qa, qb) = [ordered(k) for k in range(6)]
-    joined = (
-        span * xa + xb,
-        ga + span * gb,
-        span * (ma + float(rows) * xa) + mb,
-        na + span * (nb + float(rows) * gb),
-        ra + rb + xa * gb,
-        qa + qb + ma * gb + xa * nb,
-    )
-    for k, found in enumerate(joined):
-        chipsum[:, k * tiles : (k + 1) * tiles, :] = found
-
-    each(half, owned, lambda j: ask(j, chip, j * stride).start())
-    if_owner(lambda: None, lambda: ask(owned, chip, owned * stride).start())
+                    sums2[m, pl.ds(at_row * tiles + t, 1), :] = row
+
+    pair_up2().start()
 
     def owner_prefix():
         inbox[chip] = chipsum[owned]
@@ -229,20 +255,23 @@
             leave = span2 * leave + inbox[back, tiles : 2 * tiles, :]
         each(chips, chip, lambda h: reply(h, owned).start())
         halfedge[owned] = outbox[chip]
-        enter = part(outbox, 0)
-        leave = part(outbox, 1)
-        res_total = part(inbox, 4) + part(inbox, 0) * leave
-        rate_total = (
-            part(inbox, 5)
-            + part(inbox, 2) * leave
-            + enter * (part(inbox, 3) + float(2 * rows) * span2 * leave)
-        )
-        total[0:tiles, :] = jnp.sum(res_total, axis=0)
-        total[tiles : 2 * tiles, :] = jnp.sum(rate_total, axis=0)
-        each(ctx, me, lambda d: spread(d, mode).start())
-        answer[mode] = total[...]
-
-    if_owner(owner_prefix, lambda: reply(chip, owned).wait_recv())
+
+    if_owner(owner_prefix)
+
+    pair_up2().wait_recv()
+    (ma, mb), (na, nb), (ra, rb), (qa, qb) = [ordered(sums2, twin2, k) for k in range(4)]
+    joined = (
+        span * (ma + float(rows) * xa) + mb,
+        na + span * (nb + float(rows) * gb),
+        ra + rb + xa * gb,
+        qa + qb + ma * gb + xa * nb,
+    )
+    for k, found in enumerate(joined):
+        chipsum2[:, k * tiles : (k + 1) * tiles, :] = found
+    each(half, owned, lambda j: ask2(j, chip, j * stride).start())
+    if_owner(lambda: None, lambda: ask2(owned, chip, owned * stride).start())
+
+    if_owner(lambda: None, lambda: reply(chip, owned).wait_recv())
     each(half, owned, lambda j: reply(chip, j).wait_recv())
 
     enter = part(halfedge, 0)
@@ -254,6 +283,25 @@
     twinedge[:, 0:tiles, :] = jnp.where(first, enter_b, enter)
     twinedge[:, tiles : 2 * tiles, :] = jnp.where(first, leave, leave_a)
     pair_down().start()
+
+    def owner_totals():
+        inbox2[chip] = chipsum2[owned]
+        each(chips, chip, lambda h: ask2(owned, h, h).wait_recv())
+        span2 = spans[mode] * spans[mode]
+        enter = part(outbox, 0)
+        leave = part(outbox, 1)
+        res_total = part(inbox2, 2) + part(inbox, 0) * leave
+        rate_total = (
+            part(inbox2, 3)
+            + part(inbox2, 0) * leave
+            + enter * (part(inbox2, 1) + float(2 * rows) * span2 * leave)
+        )
+        total[0:tiles, :] = jnp.sum(res_total, axis=0)
+        total[tiles : 2 * tiles, :] = jnp.sum(rate_total, axis=0)
+        each(ctx, me, lambda d: spread(d, mode).start())
+        answer[mode] = total[...]
+
+    if_owner(owner_totals)
     pair_down().wait_recv()
 
     def finish(t):
@@ -328,13 +376,19 @@
 
     pair_up().wait_send()
     pair_down().wait_send()
+    pair_up2().wait_send()
     each(half, owned, lambda j: ask(j, chip, j * stride).wait_send())
+    each(half, owned, lambda j: ask2(j, chip, j * stride).wait_send())
 
     def owner_drain():
         each(chips, chip, lambda h: reply(h, owned).wait_send())
         each(ctx, me, lambda d: spread(d, mode).wait_send())
 
-    if_owner(owner_drain, lambda: ask(owned, chip, owned * stride).wait_send())
+    def other_drain():
+        ask(owned, chip, owned * stride).wait_send()
+        ask2(owned, chip, owned * stride).wait_send()
+
+    if_owner(owner_drain, other_drain)
 
     for p in range(1, chan):
         partner(p).wait()
@@ -343,14 +397,20 @@
 
 
 def copy_kernel(*refs):
-    count = len(refs) // 2
-    sems = refs[-1]
-    copies = [
-        pltpu.make_async_copy(refs[i], refs[count + i], sems.at[i]) for i in range(count)
+    count = (len(refs) - 2) // 3
+    staged = refs[2 * count : 3 * count]
+    inward = [
+        pltpu.make_async_copy(refs[i], staged[i], refs[-2].at[i]) for i in range(count)
     ]
-    for copy in copies:
+    outward = [
+        pltpu.make_async_copy(staged[i], refs[count + i], refs[-1].at[i]) for i in range(count)
+    ]
+    for copy in inward:
         copy.start()
-    for copy in copies:
+    for i in range(count):
+        inward[i].wait()
+        outward[i].start()
+    for copy in outward:
         copy.wait()
 
 
@@ -384,16 +444,20 @@
             buffer(tiles, modes, LANES),
             buffer(tiles, modes, LANES),
             buffer(tiles, modes, LANES),
-            buffer(2, modes, LANES),
+            buffer(2, tiles, modes, LANES),
             buffer(modes, tiles, SUBS, LANES),
             buffer(modes, tiles, SUBS, LANES),
             buffer(tiles, block, SUBS, LANES),
             buffer(tiles, block, SUBS, LANES),
             buffer(modes, tiles, LANES),
-            buffer(modes, 6 * tiles, LANES),
-            buffer(half, 6 * tiles, LANES),
-            buffer(half, 6 * tiles, LANES),
-            buffer(chips, 6 * tiles, LANES),
+            buffer(modes, 2 * tiles, LANES),
+            buffer(modes, 4 * tiles, LANES),
+            buffer(half, 2 * tiles, LANES),
+            buffer(half, 4 * tiles, LANES),
+            buffer(half, 2 * tiles, LANES),
+            buffer(half, 4 * tiles, LANES),
+            buffer(chips, 2 * tiles, LANES),
+            buffer(chips, 4 * tiles, LANES),
             buffer(chips, 2 * tiles, LANES),
             buffer(half, 2 * tiles, LANES),
             buffer(half, 2 * tiles, LANES),
@@ -403,20 +467,23 @@
             buffer(chan, SUBS, LANES),
             dma, dma, dma((half,)), dma((chips,)), dma((chips,)), dma((half,)),
             dma, dma, dma((ctx,)), dma((modes,)), dma((chan,)), dma((chan,)),
+            dma, dma, dma((half,)), dma((chips,)),
         ],
         compiler_params=pltpu.CompilerParams(collective_id=0, has_side_effects=True),
         name="hyena",
     )(query_in, key_in, value_in, grad_out, residue, decay_rate)
     anywhere = pl.BlockSpec(memory_space=pl.ANY)
-    *grads, norm = pl.pallas_call(
+    count = len(shapes) - 1
+    placed = pl.pallas_call(
         copy_kernel,
-        in_specs=[anywhere] * len(shapes),
-        out_specs=[anywhere] * len(shapes),
-        out_shape=shapes,
-        scratch_shapes=[dma((len(shapes),))],
+        in_specs=[anywhere] * count,
+        out_specs=[anywhere] * count,
+        out_shape=shapes[:count],
+        scratch_shapes=[pltpu.VMEM(leaf.shape, leaf.dtype) for leaf in shapes[:count]]
+        + [dma((count,)), dma((count,))],
         name="place",
-    )(*found)
-    return (*grads, norm.reshape(()))
+    )(*found[:count])
+    return (*placed, found[count].reshape(()))
 
 
 def solution(mesh):

time: 39 us -> 28.9 us (0.74)
  Pallas kernels: 38.2 us -> 26.3 us
  between operations: 0.64 us -> 2.4 us
    pallas_call x1, Pallas kernels: 15.7 us -> 1.79 us  [on_device(): pl.pallas_call(copy_kernel, in_specs=[anywhere] * count, out_specs=[anywh...]
    pallas_call x1, Pallas kernels: 22.5 us -> 24.5 us  [on_device(): pl.pallas_call(functools.partial(kernel, ctx, chan, rows * ctx), in_specs...]
where the time goes in v4:
time: 28.9 us; the launch traced here: 28.7 us
  Pallas kernels  26.3 us (91%)
  between operations  2.4 us (8%)
    pallas_call x1, Pallas kernels, on_device(): pl.pallas_call(functools.partial(kernel, ctx, chan, rows * ctx), in_specs...  24.5 us
    pallas_call x1, Pallas kernels, on_device(): pl.pallas_call(copy_kernel, in_specs=[anywhere] * count, out_specs=[anywh...  1.79 us

profile of v4, /device:TPU:0, one launch (start us, length us, event | category | flops | bytes accessed | tf_op | source)
XLA Modules:
  0.0 28.7 jit_solution(10506289377889393045)
XLA Ops:
  0.6 24.5 %hyena.1 = (bf16[128,512]{1,0:T(8,128)(2,1)}, bf16[128,512]{1,0:T(8,128)(2,1)}, bf16[128,512]{1,0:T(8,128)(2,1)}, f32[16,512]{1,0:T(8,128)}, f32[16,512]{1,0:T(8,128)}, /*index=5*/f32[1,1]{1,0:T(1,128)}) custom-call(bf16[128,512]{1,0:T(8,128)(2,1)} %query_ref.1, bf16[128,512]{1,0:T(8,128)(2,1)} %key_ref.1, bf16[128,512]{1,0:T(8,128)(2,1)} %value_ref.1, ...), custom_call_target="tpu_custom_call" | custom-call | tf_op jit(solution)/shard_map/hyena/pallas_call | solution.py:436
  25.2 1.8 %place.1 = (bf16[128,512]{1,0:T(8,128)(2,1)}, bf16[128,512]{1,0:T(8,128)(2,1)}, bf16[128,512]{1,0:T(8,128)(2,1)}, f32[16,512]{1,0:T(8,128)}, f32[16,512]{1,0:T(8,128)}) custom-call(bf16[128,512]{1,0:T(8,128)(2,1)} %get-tuple-element.17.refs_0_, bf16[128,512]{1,0:T(8,128)(2,1)} %get-tuple-element.18.refs_1_, bf16[128,512]{1,0:T(8,128)(2,1)} %get-tuple-element.19.refs_2_, ...), custom_call_target="tpu_custom_call" | custom-call | tf_op jit(solution)/shard_map/place/pallas_call | solution.py:477

commit v5 on v4

--- a/solution.py
+++ b/solution.py
@@ -11,13 +11,14 @@
 LANES = 128
 SUBS = 8
 GROUP = 4
+UNROLL = 16
 
 
 def kernel(
     ctx, chan, positions,
     query_ref, key_ref, value_ref, grad_ref, res_ref, rate_ref,
     gq_ref, gk_ref, gv_ref, gres_ref, grate_ref, norm_ref,
-    mixed, gmix, factors, rates, residues, lags, enters, leaves, convs, gconvs, spans,
+    mixed, gmix, factors, rates, residues, taps, lags, enters, leaves, convs, gconvs, spans,
     sums, sums2, twin, twin2, chipsum, chipsum2, inbox, inbox2, outbox, halfedge, twinedge, edges, total, answer, square,
     send0, recv0, send1, recv1, send2, recv2, send3, recv3, send4, recv4, send5, recv5,
     send6, recv6, send7, recv7,
@@ -42,7 +43,7 @@
 
     barrier = pltpu.get_barrier_semaphore()
 
-    @pl.loop(1, ctx)
+    @pl.loop(1, ctx, unroll=ctx <= UNROLL)
     def _(p):
         pl.semaphore_signal(
             barrier, inc=1, device_id=(lax.rem(me + p, ctx), mine), device_id_type=MESH
@@ -147,7 +148,7 @@
             pl.when(jnp.logical_not(owner))(otherwise)
 
     def each(count, start, act):
-        @pl.loop(1, count)
+        @pl.loop(1, count, unroll=count <= UNROLL)
         def _(p):
             act(lax.rem(start + p, count))
 
@@ -163,12 +164,11 @@
         factor = factors[t]
         res = residues[t]
         power = jnp.ones_like(factor)
-        taps = []
         lag_res = jnp.zeros_like(factor)
         lag_rate = jnp.zeros_like(factor)
         for j in range(block):
             tap = jnp.sum(res * power, axis=0, keepdims=True)
-            taps.append(jnp.broadcast_to(tap, (SUBS, LANES)))
+            taps[t, j] = jnp.broadcast_to(tap, (SUBS, LANES))
             products = x[0] * g[j]
             for i in range(1, block - j):
                 products = products + x[i] * g[i + j]
@@ -176,15 +176,6 @@
             lag_res = lag_res + term
             lag_rate = lag_rate + float(j) * term
             power = power * factor
-        for i in range(block):
-            acc = taps[0] * x[i]
-            for j in range(1, i + 1):
-                acc = acc + taps[j] * x[i - j]
-            convs[t, i] = acc
-            acc = taps[0] * g[i]
-            for j in range(1, block - i):
-                acc = acc + taps[j] * g[i + j]
-            gconvs[t, i] = acc
         lags[0, t] = lag_res
         lags[1, t] = lag_rate
 
@@ -271,6 +262,21 @@
     each(half, owned, lambda j: ask2(j, chip, j * stride).start())
     if_owner(lambda: None, lambda: ask2(owned, chip, owned * stride).start())
 
+    @pl.loop(0, tiles)
+    def _(t):
+        x = blocks_of(mixed, t)
+        g = blocks_of(gmix, t)
+        h = [taps[t, j] for j in range(block)]
+        for i in range(block):
+            acc = h[0] * x[i]
+            for j in range(1, i + 1):
+                acc = acc + h[j] * x[i - j]
+            convs[t, i] = acc
+            acc = h[0] * g[i]
+            for j in range(1, block - i):
+                acc = acc + h[j] * g[i + j]
+            gconvs[t, i] = acc
+
     if_owner(lambda: None, lambda: reply(chip, owned).wait_recv())
     each(half, owned, lambda j: reply(chip, j).wait_recv())
 
@@ -444,6 +450,7 @@
             buffer(tiles, modes, LANES),
             buffer(tiles, modes, LANES),
             buffer(tiles, modes, LANES),
+            buffer(tiles, block, SUBS, LANES),
             buffer(2, tiles, modes, LANES),
             buffer(modes, tiles, SUBS, LANES),
             buffer(modes, tiles, SUBS, LANES),

time: 28.9 us -> 28.8 us (level)
  no operation moved by 1% of the time
where the time goes in v5:
time: 28.8 us; the launch traced here: 28.6 us
  Pallas kernels  26.2 us (91%)
  between operations  2.4 us (8%)
    pallas_call x1, Pallas kernels, on_device(): pl.pallas_call(functools.partial(kernel, ctx, chan, rows * ctx), in_specs...  24.4 us
    pallas_call x1, Pallas kernels, on_device(): pl.pallas_call(copy_kernel, in_specs=[anywhere] * count, out_specs=[anywh...  1.79 us

profile of v5, /device:TPU:0, one launch (start us, length us, event | category | flops | bytes accessed | tf_op | source)
XLA Modules:
  0.0 28.6 jit_solution(14131971111970718321)
XLA Ops:
  0.6 24.4 %hyena.1 = (bf16[128,512]{1,0:T(8,128)(2,1)}, bf16[128,512]{1,0:T(8,128)(2,1)}, bf16[128,512]{1,0:T(8,128)(2,1)}, f32[16,512]{1,0:T(8,128)}, f32[16,512]{1,0:T(8,128)}, /*index=5*/f32[1,1]{1,0:T(1,128)}) custom-call(bf16[128,512]{1,0:T(8,128)(2,1)} %query_ref.1, bf16[128,512]{1,0:T(8,128)(2,1)} %key_ref.1, bf16[128,512]{1,0:T(8,128)(2,1)} %value_ref.1, ...), custom_call_target="tpu_custom_call" | custom-call | tf_op jit(solution)/shard_map/hyena/pallas_call | solution.py:442
  25.1 1.8 %place.1 = (bf16[128,512]{1,0:T(8,128)(2,1)}, bf16[128,512]{1,0:T(8,128)(2,1)}, bf16[128,512]{1,0:T(8,128)(2,1)}, f32[16,512]{1,0:T(8,128)}, f32[16,512]{1,0:T(8,128)}) custom-call(bf16[128,512]{1,0:T(8,128)(2,1)} %get-tuple-element.17.refs_0_, bf16[128,512]{1,0:T(8,128)(2,1)} %get-tuple-element.18.refs_1_, bf16[128,512]{1,0:T(8,128)(2,1)} %get-tuple-element.19.refs_2_, ...), custom_call_target="tpu_custom_call" | custom-call | tf_op jit(solution)/shard_map/place/pallas_call | solution.py:484

commit v6 on v3

--- a/solution.py
+++ b/solution.py
@@ -11,14 +11,15 @@
 LANES = 128
 SUBS = 8
 GROUP = 4
+UNROLL = 16
 
 
 def kernel(
     ctx, chan, positions,
     query_ref, key_ref, value_ref, grad_ref, res_ref, rate_ref,
     gq_ref, gk_ref, gv_ref, gres_ref, grate_ref, norm_ref,
-    mixed, gmix, factors, rates, residues, lags, enters, leaves, convs, gconvs, spans,
-    sums, twin, chipsum, inbox, outbox, halfedge, twinedge, edges, total, answer, square,
+    mixed, gmix, factors, rates, residues, taps, lags, enters, leaves, convs, gconvs, spans,
+    sums, twin, chipsum, inbox, outbox, heard, edges, total, answer, square,
     send0, recv0, send1, recv1, send2, recv2, send3, recv3, send4, recv4, send5, recv5,
 ):
     modes, channels = res_ref.shape
@@ -41,7 +42,7 @@
 
     barrier = pltpu.get_barrier_semaphore()
 
-    @pl.loop(1, ctx)
+    @pl.loop(1, ctx, unroll=ctx <= UNROLL)
     def _(p):
         pl.semaphore_signal(
             barrier, inc=1, device_id=(lax.rem(me + p, ctx), mine), device_id_type=MESH
@@ -78,12 +79,11 @@
         factor = factors[t]
         res = residues[t]
         power = jnp.ones_like(factor)
-        taps = []
         lag_res = jnp.zeros_like(factor)
         lag_rate = jnp.zeros_like(factor)
         for j in range(block):
             tap = jnp.sum(res * power, axis=0, keepdims=True)
-            taps.append(jnp.broadcast_to(tap, (SUBS, LANES)))
+            taps[t, j] = jnp.broadcast_to(tap, (SUBS, LANES))
             products = x[0] * g[j]
             for i in range(1, block - j):
                 products = products + x[i] * g[i + j]
@@ -91,17 +91,8 @@
             lag_res = lag_res + term
             lag_rate = lag_rate + float(j) * term
             power = power * factor
-        for i in range(block):
-            acc = taps[0] * x[i]
-            for j in range(1, i + 1):
-                acc = acc + taps[j] * x[i - j]
-            convs[t, i] = acc
-            acc = taps[0] * g[i]
-            for j in range(1, block - i):
-                acc = acc + taps[j] * g[i + j]
-            gconvs[t, i] = acc
-        lags[0] = lag_res
-        lags[1] = lag_rate
+        lags[0, t] = lag_res
+        lags[1, t] = lag_rate
 
         @pl.loop(0, modes // GROUP)
         def _(at):
@@ -139,8 +130,8 @@
                     down[:1],
                     jnp.sum(moment, axis=0, keepdims=True),
                     jnp.sum(gmoment, axis=0, keepdims=True),
-                    jnp.sum(cross, axis=0, keepdims=True) + lags[0, pl.ds(m, 1), :],
-                    jnp.sum(cross1, axis=0, keepdims=True) + lags[1, pl.ds(m, 1), :],
+                    jnp.sum(cross, axis=0, keepdims=True) + lags[0, t, pl.ds(m, 1), :],
+                    jnp.sum(cross1, axis=0, keepdims=True) + lags[1, t, pl.ds(m, 1), :],
                 )
                 for at_row, row in enumerate(found):
                     sums[m, pl.ds(at_row * tiles + t, 1), :] = row
@@ -155,20 +146,18 @@
         )
 
     def pair_up():
-        return remote(sums.at[other_half], twin, send0, recv0, sibling)
+        return remote(sums.at[other_half], twin.at[other_half], send0, recv0, sibling)
+
+    def pair_rest():
+        return remote(sums.at[own_half], twin.at[own_half], send3, recv3, sibling)
 
     def ask(j, slot, at):
         return remote(
             chipsum.at[j], inbox.at[slot], send1.at[j], recv1.at[slot], 2 * at + core
         )
 
-    def reply(h, slot):
-        return remote(
-            outbox.at[h], halfedge.at[slot], send2.at[h], recv2.at[slot], 2 * h + core
-        )
-
-    def pair_down():
-        return remote(twinedge, edges.at[own_half], send3, recv3, sibling)
+    def reply(d, slot):
+        return remote(outbox.at[d // 2], heard.at[slot], send2.at[d], recv2.at[slot], d)
 
     def spread(d, slot):
         return remote(total, answer.at[slot], send4.at[d], recv4.at[slot], d)
@@ -183,7 +172,7 @@
             pl.when(jnp.logical_not(owner))(otherwise)
 
     def each(count, start, act):
-        @pl.loop(1, count)
+        @pl.loop(1, count, unroll=count <= UNROLL)
         def _(p):
             act(lax.rem(start + p, count))
 
@@ -191,15 +180,16 @@
         return ref[:, k * tiles : (k + 1) * tiles, :]
 
     pair_up().start()
-    pair_up().wait_recv()
+    pair_rest().start()
     first = core == 0
     span = spans[own_half]
 
     def ordered(k):
         here = sums[own_half, k * tiles : (k + 1) * tiles, :]
-        there = part(twin, k)
+        there = twin[own_half, k * tiles : (k + 1) * tiles, :]
         return jnp.where(first, here, there), jnp.where(first, there, here)
 
+    pair_up().wait_recv()
     (xa, xb), (ga, gb), (ma, mb), (na, nb), (ra, rb), (qa, qb) = [ordered(k) for k in range(6)]
     joined = (
         span * xa + xb,
@@ -211,11 +201,25 @@
     )
     for k, found in enumerate(joined):
         chipsum[:, k * tiles : (k + 1) * tiles, :] = found
-
     each(half, owned, lambda j: ask(j, chip, j * stride).start())
     if_owner(lambda: None, lambda: ask(owned, chip, owned * stride).start())
 
-    def owner_prefix():
+    @pl.loop(0, tiles)
+    def _(t):
+        x = blocks_of(mixed, t)
+        g = blocks_of(gmix, t)
+        h = [taps[t, j] for j in range(block)]
+        for i in range(block):
+            acc = h[0] * x[i]
+            for j in range(1, i + 1):
+                acc = acc + h[j] * x[i - j]
+            convs[t, i] = acc
+            acc = h[0] * g[i]
+            for j in range(1, block - i):
+                acc = acc + h[j] * g[i + j]
+            gconvs[t, i] = acc
+
+    def owner_work():
         inbox[chip] = chipsum[owned]
         each(chips, chip, lambda h: ask(owned, h, h).wait_recv())
         span2 = spans[mode] * spans[mode]
@@ -227,8 +231,8 @@
             back = chips - 1 - h
             outbox[back, tiles : 2 * tiles, :] = leave
             leave = span2 * leave + inbox[back, tiles : 2 * tiles, :]
-        each(chips, chip, lambda h: reply(h, owned).start())
-        halfedge[owned] = outbox[chip]
+        each(ctx, me, lambda d: reply(d, mode).start())
+        heard[mode] = outbox[chip]
         enter = part(outbox, 0)
         leave = part(outbox, 1)
         res_total = part(inbox, 4) + part(inbox, 0) * leave
@@ -242,19 +246,14 @@
         each(ctx, me, lambda d: spread(d, mode).start())
         answer[mode] = total[...]
 
-    if_owner(owner_prefix, lambda: reply(chip, owned).wait_recv())
-    each(half, owned, lambda j: reply(chip, j).wait_recv())
-
-    enter = part(halfedge, 0)
-    leave = part(halfedge, 1)
-    enter_b = span * enter + xa
-    leave_a = span * leave + gb
-    edges[own_half, 0:tiles, :] = jnp.where(first, enter, enter_b)
-    edges[own_half, tiles : 2 * tiles, :] = jnp.where(first, leave_a, leave)
-    twinedge[:, 0:tiles, :] = jnp.where(first, enter_b, enter)
-    twinedge[:, tiles : 2 * tiles, :] = jnp.where(first, leave, leave_a)
-    pair_down().start()
-    pair_down().wait_recv()
+    if_owner(owner_work, lambda: reply(me, mode).wait_recv())
+    pair_rest().wait_recv()
+    each(modes, mode, lambda m: reply(me, m).wait_recv())
+
+    enter = part(heard, 0)
+    leave = part(heard, 1)
+    edges[:, 0:tiles, :] = jnp.where(first, enter, spans[...] * enter + part(twin, 0))
+    edges[:, tiles : 2 * tiles, :] = jnp.where(first, spans[...] * leave + part(twin, 1), leave)
 
     def finish(t):
         lanes = lanes_of(t)
@@ -292,7 +291,7 @@
         gk_ref[:, lanes] = (gwhole * value_ref[:, lanes].astype(f32)).astype(jnp.bfloat16)
         gv_ref[:, lanes] = (gwhole * key_ref[:, lanes].astype(f32)).astype(jnp.bfloat16)
 
-    pl.loop(0, tiles // 2)(finish)
+    pl.loop(0, tiles // 4)(finish)
 
     if_owner(lambda: None, lambda: spread(me, mode).wait_recv())
     each(modes, mode, lambda m: spread(me, m).wait_recv())
@@ -324,17 +323,20 @@
     for p in range(1, chan):
         partner(p).start()
 
-    pl.loop(tiles // 2, tiles)(finish)
+    pl.loop(tiles // 4, tiles)(finish)
 
     pair_up().wait_send()
-    pair_down().wait_send()
+    pair_rest().wait_send()
     each(half, owned, lambda j: ask(j, chip, j * stride).wait_send())
 
     def owner_drain():
-        each(chips, chip, lambda h: reply(h, owned).wait_send())
+        each(ctx, me, lambda d: reply(d, mode).wait_send())
         each(ctx, me, lambda d: spread(d, mode).wait_send())
 
-    if_owner(owner_drain, lambda: ask(owned, chip, owned * stride).wait_send())
+    def other_drain():
+        ask(owned, chip, owned * stride).wait_send()
+
+    if_owner(owner_drain, other_drain)
 
     for p in range(1, chan):
         partner(p).wait()
@@ -343,14 +345,20 @@
 
 
 def copy_kernel(*refs):
-    count = len(refs) // 2
-    sems = refs[-1]
-    copies = [
-        pltpu.make_async_copy(refs[i], refs[count + i], sems.at[i]) for i in range(count)
+    count = (len(refs) - 2) // 3
+    staged = refs[2 * count : 3 * count]
+    inward = [
+        pltpu.make_async_copy(refs[i], staged[i], refs[-2].at[i]) for i in range(count)
     ]
-    for copy in copies:
+    outward = [
+        pltpu.make_async_copy(staged[i], refs[count + i], refs[-1].at[i]) for i in range(count)
+    ]
+    for copy in inward:
         copy.start()
-    for copy in copies:
+    for i in range(count):
+        inward[i].wait()
+        outward[i].start()
+    for copy in outward:
         copy.wait()
 
 
@@ -384,39 +392,41 @@
             buffer(tiles, modes, LANES),
             buffer(tiles, modes, LANES),
             buffer(tiles, modes, LANES),
-            buffer(2, modes, LANES),
+            buffer(tiles, block, SUBS, LANES),
+            buffer(2, tiles, modes, LANES),
             buffer(modes, tiles, SUBS, LANES),
             buffer(modes, tiles, SUBS, LANES),
             buffer(tiles, block, SUBS, LANES),
             buffer(tiles, block, SUBS, LANES),
             buffer(modes, tiles, LANES),
             buffer(modes, 6 * tiles, LANES),
-            buffer(half, 6 * tiles, LANES),
+            buffer(modes, 6 * tiles, LANES),
             buffer(half, 6 * tiles, LANES),
             buffer(chips, 6 * tiles, LANES),
             buffer(chips, 2 * tiles, LANES),
-            buffer(half, 2 * tiles, LANES),
-            buffer(half, 2 * tiles, LANES),
+            buffer(modes, 2 * tiles, LANES),
             buffer(modes, 2 * tiles, LANES),
             buffer(2 * tiles, LANES),
             buffer(modes, 2 * tiles, LANES),
             buffer(chan, SUBS, LANES),
-            dma, dma, dma((half,)), dma((chips,)), dma((chips,)), dma((half,)),
+            dma, dma, dma((half,)), dma((chips,)), dma((ctx,)), dma((modes,)),
             dma, dma, dma((ctx,)), dma((modes,)), dma((chan,)), dma((chan,)),
         ],
         compiler_params=pltpu.CompilerParams(collective_id=0, has_side_effects=True),
         name="hyena",
     )(query_in, key_in, value_in, grad_out, residue, decay_rate)
     anywhere = pl.BlockSpec(memory_space=pl.ANY)
-    *grads, norm = pl.pallas_call(
+    count = len(shapes) - 1
+    placed = pl.pallas_call(
         copy_kernel,
-        in_specs=[anywhere] * len(shapes),
-        out_specs=[anywhere] * len(shapes),
-        out_shape=shapes,
-        scratch_shapes=[dma((len(shapes),))],
+        in_specs=[anywhere] * count,
+        out_specs=[anywhere] * count,
+        out_shape=shapes[:count],
+        scratch_shapes=[pltpu.VMEM(leaf.shape, leaf.dtype) for leaf in shapes[:count]]
+        + [dma((count,)), dma((count,))],
         name="place",
-    )(*found)
-    return (*grads, norm.reshape(()))
+    )(*found[:count])
+    return (*placed, found[count].reshape(()))
 
 
 def solution(mesh):

time: 39 us -> 26.8 us (0.69)
  Pallas kernels: 38.2 us -> 24.3 us
  between operations: 0.64 us -> 2.4 us
    pallas_call x1, Pallas kernels: 15.7 us -> 1.79 us  [on_device(): pl.pallas_call(copy_kernel, in_specs=[anywhere] * count, out_specs=[anywh...]
where the time goes in v6:
time: 26.8 us; the launch traced here: 26.7 us
  Pallas kernels  24.3 us (91%)
  between operations  2.4 us (9%)
    pallas_call x1, Pallas kernels, on_device(): pl.pallas_call(functools.partial(kernel, ctx, chan, rows * ctx), in_specs...  22.5 us
    pallas_call x1, Pallas kernels, on_device(): pl.pallas_call(copy_kernel, in_specs=[anywhere] * count, out_specs=[anywh...  1.79 us

profile of v6, /device:TPU:0, one launch (start us, length us, event | category | flops | bytes accessed | tf_op | source)
XLA Modules:
  0.0 26.7 jit_solution(11320904705099068673)
XLA Ops:
  0.6 22.5 %hyena.1 = (bf16[128,512]{1,0:T(8,128)(2,1)}, bf16[128,512]{1,0:T(8,128)(2,1)}, bf16[128,512]{1,0:T(8,128)(2,1)}, f32[16,512]{1,0:T(8,128)}, f32[16,512]{1,0:T(8,128)}, /*index=5*/f32[1,1]{1,0:T(1,128)}) custom-call(bf16[128,512]{1,0:T(8,128)(2,1)} %query_ref.1, bf16[128,512]{1,0:T(8,128)(2,1)} %key_ref.1, bf16[128,512]{1,0:T(8,128)(2,1)} %value_ref.1, ...), custom_call_target="tpu_custom_call" | custom-call | tf_op jit(solution)/shard_map/hyena/pallas_call | solution.py:384
  23.1 1.8 %place.1 = (bf16[128,512]{1,0:T(8,128)(2,1)}, bf16[128,512]{1,0:T(8,128)(2,1)}, bf16[128,512]{1,0:T(8,128)(2,1)}, f32[16,512]{1,0:T(8,128)}, f32[16,512]{1,0:T(8,128)}) custom-call(bf16[128,512]{1,0:T(8,128)(2,1)} %get-tuple-element.17.refs_0_, bf16[128,512]{1,0:T(8,128)(2,1)} %get-tuple-element.18.refs_1_, bf16[128,512]{1,0:T(8,128)(2,1)} %get-tuple-element.19.refs_2_, ...), custom_call_target="tpu_custom_call" | custom-call | tf_op jit(solution)/shard_map/place/pallas_call | solution.py:420

commit v7 on v6

--- a/solution.py
+++ b/solution.py
@@ -18,7 +18,7 @@
     ctx, chan, positions,
     query_ref, key_ref, value_ref, grad_ref, res_ref, rate_ref,
     gq_ref, gk_ref, gv_ref, gres_ref, grate_ref, norm_ref,
-    mixed, gmix, factors, rates, residues, taps, lags, enters, leaves, convs, gconvs, spans,
+    mixed, gmix, factors, rates, residues, lags, enters, leaves, convs, gconvs, spans,
     sums, twin, chipsum, inbox, outbox, heard, edges, total, answer, square,
     send0, recv0, send1, recv1, send2, recv2, send3, recv3, send4, recv4, send5, recv5,
 ):
@@ -77,13 +77,10 @@
         x = blocks_of(mixed, t)
         g = blocks_of(gmix, t)
         factor = factors[t]
-        res = residues[t]
         power = jnp.ones_like(factor)
         lag_res = jnp.zeros_like(factor)
         lag_rate = jnp.zeros_like(factor)
         for j in range(block):
-            tap = jnp.sum(res * power, axis=0, keepdims=True)
-            taps[t, j] = jnp.broadcast_to(tap, (SUBS, LANES))
             products = x[0] * g[j]
             for i in range(1, block - j):
                 products = products + x[i] * g[i + j]
@@ -208,7 +205,13 @@
     def _(t):
         x = blocks_of(mixed, t)
         g = blocks_of(gmix, t)
-        h = [taps[t, j] for j in range(block)]
+        factor = factors[t]
+        power = residues[t]
+        h = []
+        for j in range(block):
+            tap = jnp.sum(power, axis=0, keepdims=True)
+            h.append(jnp.broadcast_to(tap, (SUBS, LANES)))
+            power = power * factor
         for i in range(block):
             acc = h[0] * x[i]
             for j in range(1, i + 1):
@@ -258,30 +261,39 @@
     def finish(t):
         lanes = lanes_of(t)
 
-        def body(at, held):
-            conv, gconv = list(held[0]), list(held[1])
+        def forward(at, held):
+            conv = list(held)
             for lane in range(GROUP):
                 m = at * GROUP + lane
                 f = row_of(factors, m, t)
                 rate = rates[t, pl.ds(m, 1), :]
                 res = residues[t, pl.ds(m, 1), :]
                 into = edges[m, pl.ds(t, 1), :]
-                out = edges[m, pl.ds(tiles + t, 1), :]
                 z = res * (enters[m, t] + jnp.exp(-rate * before) * into)
-                y = (res * f) * (leaves[m, t] + jnp.exp(-rate * after) * out)
                 for i in range(block):
                     conv[i] = conv[i] + z
-                    gconv[block - 1 - i] = gconv[block - 1 - i] + y
                     if i < block - 1:
                         z = z * f
+            return tuple(conv)
+
+        def backward(at, held):
+            gconv = list(held)
+            for lane in range(GROUP):
+                m = at * GROUP + lane
+                f = row_of(factors, m, t)
+                rate = rates[t, pl.ds(m, 1), :]
+                res = residues[t, pl.ds(m, 1), :]
+                out = edges[m, pl.ds(tiles + t, 1), :]
+                y = (res * f) * (leaves[m, t] + jnp.exp(-rate * after) * out)
+                for i in range(block - 1, -1, -1):
+                    gconv[i] = gconv[i] + y
+                    if i > 0:
                         y = y * f
-            return tuple(conv), tuple(gconv)
-
-        start = (
-            tuple(convs[t, i] for i in range(block)),
-            tuple(gconvs[t, i] for i in range(block)),
-        )
-        conv, gconv = lax.fori_loop(0, modes // GROUP, body, start)
+            return tuple(gconv)
+
+        steps = modes // GROUP
+        conv = lax.fori_loop(0, steps, forward, tuple(convs[t, i] for i in range(block)))
+        gconv = lax.fori_loop(0, steps, backward, tuple(gconvs[t, i] for i in range(block)))
         for i in range(block):
             mixed[t, pl.ds(i, SUBS, stride=block), :] = conv[i]
             gmix[t, pl.ds(i, SUBS, stride=block), :] = gconv[i]
@@ -392,7 +404,6 @@
             buffer(tiles, modes, LANES),
             buffer(tiles, modes, LANES),
             buffer(tiles, modes, LANES),
-            buffer(tiles, block, SUBS, LANES),
             buffer(2, tiles, modes, LANES),
             buffer(modes, tiles, SUBS, LANES),
             buffer(modes, tiles, SUBS, LANES),

time: 26.8 us -> 26.8 us (level)
  no operation moved by 1% of the time
where the time goes in v7:
time: 26.8 us; the launch traced here: 26.7 us
  Pallas kernels  24.3 us (91%)
  between operations  2.4 us (9%)
    pallas_call x1, Pallas kernels, on_device(): pl.pallas_call(functools.partial(kernel, ctx, chan, rows * ctx), in_specs...  22.5 us
    pallas_call x1, Pallas kernels, on_device(): pl.pallas_call(copy_kernel, in_specs=[anywhere] * count, out_specs=[anywh...  1.79 us

profile of v7, /device:TPU:0, one launch (start us, length us, event | category | flops | bytes accessed | tf_op | source)
XLA Modules:
  0.0 26.7 jit_solution(7660469398785905086)
XLA Ops:
  0.6 22.5 %hyena.1 = (bf16[128,512]{1,0:T(8,128)(2,1)}, bf16[128,512]{1,0:T(8,128)(2,1)}, bf16[128,512]{1,0:T(8,128)(2,1)}, f32[16,512]{1,0:T(8,128)}, f32[16,512]{1,0:T(8,128)}, /*index=5*/f32[1,1]{1,0:T(1,128)}) custom-call(bf16[128,512]{1,0:T(8,128)(2,1)} %query_ref.1, bf16[128,512]{1,0:T(8,128)(2,1)} %key_ref.1, bf16[128,512]{1,0:T(8,128)(2,1)} %value_ref.1, ...), custom_call_target="tpu_custom_call" | custom-call | tf_op jit(solution)/shard_map/hyena/pallas_call | solution.py:396
  23.1 1.8 %place.1 = (bf16[128,512]{1,0:T(8,128)(2,1)}, bf16[128,512]{1,0:T(8,128)(2,1)}, bf16[128,512]{1,0:T(8,128)(2,1)}, f32[16,512]{1,0:T(8,128)}, f32[16,512]{1,0:T(8,128)}) custom-call(bf16[128,512]{1,0:T(8,128)(2,1)} %get-tuple-element.17.refs_0_, bf16[128,512]{1,0:T(8,128)(2,1)} %get-tuple-element.18.refs_1_, bf16[128,512]{1,0:T(8,128)(2,1)} %get-tuple-element.19.refs_2_, ...), custom_call_target="tpu_custom_call" | custom-call | tf_op jit(solution)/shard_map/place/pallas_call | solution.py:431

commit v8 on v7

--- a/solution.py
+++ b/solution.py
@@ -303,7 +303,6 @@
         gk_ref[:, lanes] = (gwhole * value_ref[:, lanes].astype(f32)).astype(jnp.bfloat16)
         gv_ref[:, lanes] = (gwhole * key_ref[:, lanes].astype(f32)).astype(jnp.bfloat16)
 
-    pl.loop(0, tiles // 4)(finish)
 
     if_owner(lambda: None, lambda: spread(me, mode).wait_recv())
     each(modes, mode, lambda m: spread(me, m).wait_recv())
@@ -335,7 +334,7 @@
     for p in range(1, chan):
         partner(p).start()
 
-    pl.loop(tiles // 4, tiles)(finish)
+    pl.loop(0, tiles)(finish)
 
     pair_up().wait_send()
     pair_rest().wait_send()

time: 26.8 us -> 26.8 us (level)
  no operation moved by 1% of the time
where the time goes in v8:
time: 26.8 us; the launch traced here: 26.7 us
  Pallas kernels  24.3 us (91%)
  between operations  2.4 us (9%)
    pallas_call x1, Pallas kernels, on_device(): pl.pallas_call(functools.partial(kernel, ctx, chan, rows * ctx), in_specs...  22.5 us
    pallas_call x1, Pallas kernels, on_device(): pl.pallas_call(copy_kernel, in_specs=[anywhere] * count, out_specs=[anywh...  1.79 us

profile of v8, /device:TPU:0, one launch (start us, length us, event | category | flops | bytes accessed | tf_op | source)
XLA Modules:
  0.0 26.7 jit_solution(15568120754019295402)
XLA Ops:
  0.6 22.5 %hyena.1 = (bf16[128,512]{1,0:T(8,128)(2,1)}, bf16[128,512]{1,0:T(8,128)(2,1)}, bf16[128,512]{1,0:T(8,128)(2,1)}, f32[16,512]{1,0:T(8,128)}, f32[16,512]{1,0:T(8,128)}, /*index=5*/f32[1,1]{1,0:T(1,128)}) custom-call(bf16[128,512]{1,0:T(8,128)(2,1)} %query_ref.1, bf16[128,512]{1,0:T(8,128)(2,1)} %key_ref.1, bf16[128,512]{1,0:T(8,128)(2,1)} %value_ref.1, ...), custom_call_target="tpu_custom_call" | custom-call | tf_op jit(solution)/shard_map/hyena/pallas_call | solution.py:395
  23.1 1.8 %place.1 = (bf16[128,512]{1,0:T(8,128)(2,1)}, bf16[128,512]{1,0:T(8,128)(2,1)}, bf16[128,512]{1,0:T(8,128)(2,1)}, f32[16,512]{1,0:T(8,128)}, f32[16,512]{1,0:T(8,128)}) custom-call(bf16[128,512]{1,0:T(8,128)(2,1)} %get-tuple-element.17.refs_0_, bf16[128,512]{1,0:T(8,128)(2,1)} %get-tuple-element.18.refs_1_, bf16[128,512]{1,0:T(8,128)(2,1)} %get-tuple-element.19.refs_2_, ...), custom_call_target="tpu_custom_call" | custom-call | tf_op jit(solution)/shard_map/place/pallas_call | solution.py:430
